TPU v7x, 256 devices: a whole 4x4x8 slice. The times are simulated.
256 devices in a mesh: dp: 64 (over x, z, core), sp: 4 (over y).
Axes of the slice: x: 4, y: 4, z: 8, core: 2. Of those that a mesh axis runs over, the one named last changes fastest.
Arguments:
- base_query: bfloat16 [64, 1024, 4096], P('dp', 'sp'), may hold values from -8 to 8
- base_key: bfloat16 [64, 1024, 512], P('dp', 'sp'), may hold values from -8 to 8
- reference_value_rows: bfloat16 [64, 1024, 512], P('dp', 'sp'), may hold values from -6 to 6
- actor_query: bfloat16 [64, 1024, 4096], P('dp', 'sp'), may hold values from -8 to 8
- actor_key: bfloat16 [64, 1024, 512], P('dp', 'sp'), may hold values from -8 to 8
- actor_value_rows: bfloat16 [64, 1024, 512], P('dp', 'sp'), may hold values from -6 to 6
- segment_labels: int32 [64, 1024], P('dp', 'sp'), may hold values from 0 to 2, never falling along the last dimension, each value on 1 to 512 neighbouring positions
- shard_plan: int32 [64], replicated, may hold values from 0 to 63, each once
Outputs:
- base_output: bfloat16 [64, 1024, 4096], P('dp', 'sp')
- actor_output: bfloat16 [64, 1024, 4096], P('dp', 'sp')
Inputs may be any that keep to these rules, and one draw needn't show every extreme that they name: `segment_labels`: along an owner's rows the labels never decrease; a response has 1 to 512 rows, and some response has exactly 512. `shard_plan`: each group is named by exactly one owner.
All inputs are finite; a program needn't handle non-finite values.
Results may differ from a plain program's by a relative error of at most 0.0079.
Values may be sent and summed in bfloat16 or wider, within the bound.
No kernel may reach another device: no remote copies, remote signals or barrier semaphores. Data moves between devices by JAX's collectives and lax.ppermute only.
A program may use at most 128 MiB of HBM per device.

v0:
```python
import functools
import math

import jax
import jax.numpy as jnp
import numpy as np
from jax import lax
from jax.experimental import pallas as pl
from jax.experimental.pallas import tpu as pltpu
from jax.sharding import PartitionSpec as P

QUERY_HEADS = 32
KEY_VALUE_HEADS = 4
HEAD_SIZE = 128
GROUP = QUERY_HEADS // KEY_VALUE_HEADS
SEGS = 3
THETA = 1000000.0
ROWS = 256
OWNERS = 64
LEAD = 1
SCALE = math.log2(math.e) / math.sqrt(HEAD_SIZE)
MASKED = -1e30
BF = jnp.bfloat16
F32 = jnp.float32


def angle_tables():
    half = HEAD_SIZE // 2
    rate = THETA ** (-2.0 * np.arange(half) / HEAD_SIZE)
    angle = np.arange(3 * ROWS)[:, None] * np.concatenate([rate, rate])[None, :]
    return np.cos(angle).astype(np.float32), np.sin(angle).astype(np.float32)


def pack_first_kernel(k_ref, v_ref, lab_ref, first_ref, rest_ref):
    width = LEAD * 256
    for c in range(KEY_VALUE_HEADS):
        k = k_ref[:, c * 128 : (c + 1) * 128]
        v = v_ref[:, c * 128 : (c + 1) * 128]
        if c < LEAD:
            first_ref[0:ROWS, c * 256 : c * 256 + 128] = k
            first_ref[0:ROWS, c * 256 + 128 : c * 256 + 256] = v
        else:
            rest_ref[:, (c - LEAD) * 256 : (c - LEAD) * 256 + 128] = k
            rest_ref[:, (c - LEAD) * 256 + 128 : (c - LEAD) * 256 + 256] = v
    along = (lab_ref[...] + 1).astype(F32)
    down = jnp.transpose(jnp.broadcast_to(along, (128, ROWS)))
    first_ref[0:ROWS, width : width + 128] = down.astype(BF)
    first_ref[ROWS : ROWS + 16, :] = jnp.zeros((16, width + 128), BF)
    first_ref[ROWS : ROWS + 16, 0:ROWS] = jnp.broadcast_to(along, (16, ROWS)).astype(BF)


def pack_first(k, v, labels):
    return pl.pallas_call(
        pack_first_kernel,
        out_shape=(
            jax.ShapeDtypeStruct((ROWS + 16, LEAD * 256 + 128), BF),
            jax.ShapeDtypeStruct((ROWS, (KEY_VALUE_HEADS - LEAD) * 256), BF),
        ),
        compiler_params=pltpu.CompilerParams(vmem_limit_bytes=16 << 20),
    )(k, v, labels)


def pack_plain_kernel(k_ref, v_ref, out_ref):
    for c in range(KEY_VALUE_HEADS):
        out_ref[:, c * 256 : c * 256 + 128] = k_ref[:, c * 128 : (c + 1) * 128]
        out_ref[:, c * 256 + 128 : c * 256 + 256] = v_ref[:, c * 128 : (c + 1) * 128]


def pack_plain(k, v):
    return pl.pallas_call(
        pack_plain_kernel,
        out_shape=jax.ShapeDtypeStruct((ROWS, KEY_VALUE_HEADS * 256), BF),
        compiler_params=pltpu.CompilerParams(vmem_limit_bytes=16 << 20),
    )(k, v)


def from_previous(x, size, step):
    return lax.ppermute(x, "sp", [(i, i + step) for i in range(size - step)])


def rotate(x, cosine, sine):
    x = x.astype(F32)
    return (x * cosine + pltpu.roll(x, HEAD_SIZE // 2, 1) * sine).astype(BF)


def attend_kernel(
    pieces,
    q_ref,
    kv0_ref,
    kv1_ref,
    kv2_ref,
    down0_ref,
    down1_ref,
    down2_ref,
    along0_ref,
    along1_ref,
    along2_ref,
    cos_ref,
    sin_ref,
    out_ref,
    turn_cos,
    turn_sin,
    bias_near,
    bias_ends,
):
    within = lax.broadcasted_iota(jnp.int32, (ROWS, ROWS), 1) <= lax.broadcasted_iota(
        jnp.int32, (ROWS, ROWS), 0
    )

    @pl.when(pl.program_id(0) == 0)
    def _():
        along = [ref[0:1, :].astype(F32) for ref in (along2_ref, along1_ref, along0_ref)]
        down = [ref[...].astype(F32) for ref in (down2_ref, down1_ref, down0_ref)]
        place = lax.broadcasted_iota(jnp.int32, (1, ROWS), 1)
        starts = []
        for label in range(1, SEGS + 1):
            least = jnp.full((1, ROWS), 3 * ROWS - 1, jnp.int32)
            for b in range(3):
                least = jnp.minimum(
                    least, jnp.where(along[b] == label, place + b * ROWS, 3 * ROWS - 1)
                )
            starts.append(jnp.min(least))
        start_cos = [cos_ref[pl.ds(s, 1), :] for s in starts]
        start_sin = [sin_ref[pl.ds(s, 1), :] for s in starts]
        sign = jnp.where(
            lax.broadcasted_iota(jnp.int32, (1, HEAD_SIZE), 1) < HEAD_SIZE // 2, -1.0, 1.0
        )
        for b in range(3):
            rows = pl.ds(b * ROWS, ROWS)
            first, second = down[b] == 1, down[b] == 2
            sc = jnp.where(first, start_cos[0], jnp.where(second, start_cos[1], start_cos[2]))
            ss = jnp.where(first, start_sin[0], jnp.where(second, start_sin[1], start_sin[2]))
            ic, isn = cos_ref[rows, :], sin_ref[rows, :]
            turn_cos[rows, :] = ic * sc + isn * ss
            turn_sin[rows, :] = (isn * sc - ic * ss) * sign
        own = jnp.concatenate([down[2], down[2]], axis=1)
        bias_near[...] = jnp.where(along[1] == own, 0.0, MASKED)
        bias_ends[...] = jnp.where(jnp.where(within, along[2], along[0]) == own, 0.0, MASKED)

    keys, values = [], []
    ones = jnp.ones((ROWS, HEAD_SIZE), BF)
    for b, ref in enumerate((kv2_ref, kv1_ref, kv0_ref)):
        rows = pl.ds(b * ROWS, ROWS)
        keys.append(rotate(ref[0:ROWS, 0:128], turn_cos[rows, :], turn_sin[rows, :]))
        values.append(jnp.concatenate([ref[0:ROWS, 128:256], ones], axis=1))
    keys = jnp.concatenate(keys, axis=0)
    values = jnp.concatenate(values, axis=0)
    own_cos = turn_cos[pl.ds(2 * ROWS, ROWS), :]
    own_sin = turn_sin[pl.ds(2 * ROWS, ROWS), :]
    for h in range(GROUP):
        q = rotate(q_ref[:, h * 128 : (h + 1) * 128], own_cos, own_sin)
        s = lax.dot_general(q, keys, (((1,), (1,)), ((), ())), preferred_element_type=F32)
        ends = jnp.where(within, s[:, 2 * ROWS :], s[:, :ROWS]) * SCALE + bias_ends[...]
        near = s[:, ROWS : 2 * ROWS] * SCALE + bias_near[...]
        peak = jnp.max(jnp.maximum(ends, near), axis=1, keepdims=True)
        ends = jnp.exp2(ends - peak)
        near = jnp.exp2(near - peak).astype(BF)
        inner = jnp.where(within, ends, 0.0).astype(BF)
        outer = jnp.where(within, 0.0, ends).astype(BF)
        weights = jnp.concatenate([outer, near, inner], axis=1)
        o = jnp.dot(weights, values, preferred_element_type=F32)
        o = (o[:, :128] / o[:, 128:]).astype(BF)
        if pieces:
            lanes = slice((h % 2) * 128, (h % 2) * 128 + 128)
            out_ref[:, h // 2, :, lanes] = o.reshape(16, 16, 128)
        else:
            out_ref[:, h * 128 : (h + 1) * 128] = o


def attend(pieces, q, first, count, kvs, lab, tables):
    width = LEAD * 256
    specs = [pl.BlockSpec((ROWS, GROUP * 128), lambda c: (0, c + first))]
    specs += [pl.BlockSpec((ROWS, 256), lambda c: (0, c))] * 3
    specs += [pl.BlockSpec((ROWS, 128), lambda c: (0, width // 128))] * 3
    specs += [pl.BlockSpec((16, ROWS), lambda c: (ROWS // 16, 0))] * 3
    specs += [pl.BlockSpec((3 * ROWS, HEAD_SIZE), lambda c: (0, 0))] * 2
    if pieces:
        out_shape = jax.ShapeDtypeStruct((16, 4, 16, count * 256), BF)
        out_spec = pl.BlockSpec((16, 4, 16, 256), lambda c: (0, 0, 0, c))
    else:
        out_shape = jax.ShapeDtypeStruct((ROWS, QUERY_HEADS * HEAD_SIZE), BF)
        out_spec = pl.BlockSpec((ROWS, GROUP * 128), lambda c: (0, c + first))
    return pl.pallas_call(
        functools.partial(attend_kernel, pieces),
        grid=(count,),
        in_specs=specs,
        out_specs=out_spec,
        out_shape=out_shape,
        scratch_shapes=[
            pltpu.VMEM((3 * ROWS, HEAD_SIZE), F32),
            pltpu.VMEM((3 * ROWS, HEAD_SIZE), F32),
            pltpu.VMEM((ROWS, ROWS), F32),
            pltpu.VMEM((ROWS, ROWS), F32),
        ],
        compiler_params=pltpu.CompilerParams(vmem_limit_bytes=32 << 20),
        cost_estimate=pl.CostEstimate(
            flops=count * GROUP * 4 * ROWS * 3 * ROWS * HEAD_SIZE,
            bytes_accessed=count * ROWS * (GROUP * 256 * 2 + 3 * 512),
            transcendentals=count * GROUP * ROWS * 2 * ROWS,
        ),
    )(q, *kvs, *lab, *lab, *tables)


def pick_kernel(plan_ref, lead_ref, rest_ref, out_ref):
    width = LEAD * 256

    def one(u, carry):
        g = plan_ref[u]
        out_ref[g, :, 0:width] = lead_ref[u]
        out_ref[g, :, width:1024] = rest_ref[u]
        return carry

    lax.fori_loop(0, OWNERS, one, 0, unroll=8)


def pick(plan, lead, rest):
    whole = pl.BlockSpec(memory_space=pltpu.VMEM)
    return pl.pallas_call(
        pick_kernel,
        in_specs=[pl.BlockSpec(memory_space=pltpu.SMEM), whole, whole],
        out_specs=whole,
        out_shape=jax.ShapeDtypeStruct((OWNERS, 16, 1024), BF),
        compiler_params=pltpu.CompilerParams(vmem_limit_bytes=16 << 20),
    )(plan, lead, rest)


def lay_kernel(in_ref, out_ref):
    for cb in range(4):
        out_ref[:, :, cb * 256 : (cb + 1) * 256] = in_ref[:, cb]


def lay(arrived):
    out = pl.pallas_call(
        lay_kernel,
        grid=(KEY_VALUE_HEADS,),
        in_specs=[pl.BlockSpec((16, 4, 16, 256), lambda c: (0, 0, 0, c))],
        out_specs=pl.BlockSpec((16, 16, 1024), lambda c: (0, 0, c)),
        out_shape=jax.ShapeDtypeStruct((16, 16, 4096), BF),
        compiler_params=pltpu.CompilerParams(vmem_limit_bytes=16 << 20),
    )(arrived.reshape(16, 4, 16, 1024))
    return out.reshape(ROWS, 4096)


def swap(x):
    return lax.all_to_all(x, "dp", split_axis=0, concat_axis=0, tiled=True)


def per_device(bq, bk, bv, aq, ak, av, labels, plan):
    size = lax.axis_size("sp")
    bq, bk, bv, aq, ak, av = (t[0] for t in (bq, bk, bv, aq, ak, av))
    tables = tuple(jnp.asarray(t) for t in angle_tables())

    head, rest = pack_first(ak, av, labels)
    head1, head2 = (from_previous(head, size, s) for s in (1, 2))
    lab = (head, head1, head2)
    lead = attend(True, aq, 0, LEAD, lab, lab, tables)
    lead = swap(lead.reshape(OWNERS, 16, LEAD * 256))

    rest1, rest2 = (from_previous(rest, size, s) for s in (1, 2))
    others = KEY_VALUE_HEADS - LEAD
    other = attend(True, aq, LEAD, others, (rest, rest1, rest2), lab, tables)
    other = swap(other.reshape(OWNERS, 16, others * 256))

    base = pack_plain(bk, bv)
    base1, base2 = (from_previous(base, size, s) for s in (1, 2))
    base_output = attend(False, bq, 0, KEY_VALUE_HEADS, (base, base1, base2), lab, tables)

    arrived = swap(pick(plan, lead, other))
    return base_output[None], lay(arrived)[None]


def solution(mesh):
    rows = P("dp", "sp", None)
    return jax.shard_map(
        per_device,
        mesh=mesh,
        in_specs=(rows, rows, rows, rows, rows, rows, P("dp", "sp"), P()),
        out_specs=(rows, rows),
        check_vma=False,
    )
```

profile of v0, /device:TPU:1, one launch (start us, length us, event | category | flops | bytes accessed | tf_op | source)
XLA Modules:
  0.0 179.8 jit_solution(6501090969804881953)
XLA Ops:
  0.6 0.0 copy-start.10
  0.6 0.9 copy-done.10
  1.6 0.0 copy-start.11
  1.6 0.9 copy-done.11
  2.5 0.0 copy-start.14
  2.5 0.7 copy-done.14
  3.2 0.1 shard_map.114
  3.3 0.0 copy-start.17
  3.3 0.7 copy-done.17
  4.1 4.0 %collective-permute-start.2 = (bf16[272,384]{1,0:T(8,128)(2,1)S(1)}, bf16[272,384]{1,0:T(8,128)(2,1)S(1)}, u32[]{:S(2)}, u32[]{:S(2)}) collective-permute-start(bf16[272,384]{1,0:T(8,128)(2,1)S(1)} %get-tuple-element.4.down0_ref.along0_ref.kv0_ref), channel_id=1, source_target_pairs={{0,1},{1,2},{2,3},{4,5},{5,6},{6,7},{8,9},{9,10},{10,11},{12,13},{... | collective-permute-start | bytes 626696 | tf_op jit(solution)/shard_map/ppermute | solution.py:78
  8.1 4.5 %collective-permute-start.3 = (bf16[272,384]{1,0:T(8,128)(2,1)S(1)}, bf16[272,384]{1,0:T(8,128)(2,1)S(1)}, u32[]{:S(2)}, u32[]{:S(2)}) collective-permute-start(bf16[272,384]{1,0:T(8,128)(2,1)S(1)} %get-tuple-element.4.down0_ref.along0_ref.kv0_ref), channel_id=1, source_target_pairs={{0,2},{1,3},{4,6},{5,7},{8,10},{9,11},{12,14},{13,15},{16,18},{17,... | collective-permute-start | bytes 626696 | tf_op jit(solution)/shard_map/ppermute | solution.py:78
  12.6 0.0 collective-permute-done.2.down1_ref.along1_ref.kv1_ref
  12.7 3.5 %collective-permute-done.3.down2_ref.along2_ref.kv2_ref = bf16[272,384]{1,0:T(8,128)(2,1)S(1)} collective-permute-done((bf16[272,384]{1,0:T(8,128)(2,1)S(1)}, bf16[272,384]{1,0:T(8,128)(2,1)S(1)}, u32[]{:S(2)}, u32[]{:S(2)}) %collective-permute-start.3) | collective-permute-done | bytes 208928 | tf_op jit(solution)/shard_map/ppermute | solution.py:78
  16.1 0.0 copy-start.1
  16.1 1.6 copy-done.1
  17.7 0.0 copy-start.4
  17.7 1.0 copy-done.4
  18.7 0.0 copy-start.7
  18.7 1.0 copy-done.7
  19.7 0.0 copy-start.2
  19.7 3.7 %shard_map.116 = bf16[16,4,16,256]{3,2,1,0:T(8,128)(2,1)} custom-call(bf16[256,4096]{1,0:T(8,128)(2,1)S(1)} %bitcast.12, bf16[272,384]{1,0:T(8,128)(2,1)S(1)} %get-tuple-element.4.down0_ref.along0_ref.kv0_ref, bf16[272,384]{1,0:T(8,128)(2,1)S(1)} %collective-permute-done.2.down1_ref.along1_ref.kv1_ref, ...), custom_call_target="tpu_custom_call" | custom-call | flops 805306368 | bytes 1441792 | tf_op jit(solution)/shard_map/pallas_call | solution.py:183
  23.4 13.3 %all-to-all-start = ((bf16[64,16,256]{2,1,0:T(8,128)(2,1)}), bf16[64,16,256]{2,1,0:T(8,128)(2,1)S(1)}, u32[]{:S(2)}, u32[]{:S(2)}) async-start(bf16[64,16,256]{2,1,0:T(8,128)(2,1)} %bitcast.7), calls=%async_computation | async-start | bytes 1048576 | tf_op jit(solution)/shard_map/all_to_all | solution.py:245
  36.7 1.3 collective-permute-start.4
  38.1 6.3 %collective-permute-start.5 = (bf16[256,768]{1,0:T(8,128)(2,1)}, bf16[256,768]{1,0:T(8,128)(2,1)S(1)}, u32[]{:S(2)}, u32[]{:S(2)}) collective-permute-start(bf16[256,768]{1,0:T(8,128)(2,1)} %copy-done.17), channel_id=1, source_target_pairs={{0,2},{1,3},{4,6},{5,7},{8,10},{9,11},{12,14},{13,15},{16,18},{17,... | collective-permute-start | bytes 1179656 | tf_op jit(solution)/shard_map/ppermute | solution.py:78
  44.4 2.3 %collective-permute-done.4.kv1_ref = bf16[256,768]{1,0:T(8,128)(2,1)S(1)} collective-permute-done((bf16[256,768]{1,0:T(8,128)(2,1)}, bf16[256,768]{1,0:T(8,128)(2,1)S(1)}, u32[]{:S(2)}, u32[]{:S(2)}) %collective-permute-start.4) | collective-permute-done | bytes 393248 | tf_op jit(solution)/shard_map/ppermute | solution.py:78
  46.7 8.5 %collective-permute-done.5.kv2_ref = bf16[256,768]{1,0:T(8,128)(2,1)S(1)} collective-permute-done((bf16[256,768]{1,0:T(8,128)(2,1)}, bf16[256,768]{1,0:T(8,128)(2,1)S(1)}, u32[]{:S(2)}, u32[]{:S(2)}) %collective-permute-start.5) | collective-permute-done | bytes 393248 | tf_op jit(solution)/shard_map/ppermute | solution.py:78
  55.2 0.0 copy-done.2
  55.2 0.0 copy-start.5
  55.2 1.0 copy-done.5
  56.2 0.0 copy-start.8
  56.2 1.0 copy-done.8
  57.1 0.0 copy-start.18
  57.2 1.0 copy-done.18
  58.1 8.0 %shard_map.117 = bf16[16,4,16,768]{3,2,1,0:T(8,128)(2,1)S(1)} custom-call(bf16[256,4096]{1,0:T(8,128)(2,1)S(1)} %bitcast.13, bf16[256,768]{1,0:T(8,128)(2,1)S(1)} %copy-done.18, bf16[256,768]{1,0:T(8,128)(2,1)S(1)} %collective-permute-done.4.kv1_ref, bf16[256,768]{1,0:T(8,128)(2,1)S(1)} %collective-permute-done.5.kv2_ref, ...), custom_call_target="tpu_custom_call" | custom-call | flops 2415919104 | bytes 4325376 | tf_op jit(solution)/shard_map/pallas_call | solution.py:183
  66.1 0.0 copy-start.3
  66.1 1.1 copy-done.3
  67.3 0.0 copy-start.15
  67.3 0.0 all-to-all-done.lead_ref
  67.3 50.9 %all_to_all.15.rest_ref = bf16[64,16,768]{2,1,0:T(8,128)(2,1)S(1)} all-to-all(bf16[64,16,768]{2,1,0:T(8,128)(2,1)} %bitcast.14), channel_id=1, replica_groups=mesh['dp'=64,'sp'=4] {'dp'}, dimensions={0} | all-to-all | bytes 3145728 | tf_op jit(solution)/shard_map/all_to_all | solution.py:245
  118.1 0.0 copy-done.15
  118.1 0.8 shard_map.118
  118.9 0.0 copy-start
  118.9 1.3 copy-done
  120.2 0.0 copy-start.12
  120.2 6.3 %all-to-all-start.2 = ((bf16[64,16,1024]{2,1,0:T(8,128)(2,1)}), bf16[64,16,1024]{2,1,0:T(8,128)(2,1)S(1)}, u32[]{:S(2)}, u32[]{:S(2)}) async-start(bf16[64,16,1024]{2,1,0:T(8,128)(2,1)} %copy-done), calls=%async_computation.2 | async-start | bytes 4194304 | tf_op jit(solution)/shard_map/all_to_all | solution.py:245
  126.5 0.0 copy-done.12
  126.5 0.0 copy-start.13
  126.5 0.9 copy-done.13
  127.4 0.1 shard_map.113.kv0_ref
  127.6 5.9 %collective-permute-start = (bf16[256,1024]{1,0:T(8,128)(2,1)S(1)}, bf16[256,1024]{1,0:T(8,128)(2,1)S(1)}, u32[]{:S(2)}, u32[]{:S(2)}) collective-permute-start(bf16[256,1024]{1,0:T(8,128)(2,1)S(1)} %shard_map.113.kv0_ref), channel_id=1, source_target_pairs={{0,1},{1,2},{2,3},{4,5},{5,6},{6,7},{8,9},{9,10},{10,11},{12,13},{... | collective-permute-start | bytes 1572872 | tf_op jit(solution)/shard_map/ppermute | solution.py:78
  133.5 4.5 %collective-permute-start.1 = (bf16[256,1024]{1,0:T(8,128)(2,1)S(1)}, bf16[256,1024]{1,0:T(8,128)(2,1)S(1)}, u32[]{:S(2)}, u32[]{:S(2)}) collective-permute-start(bf16[256,1024]{1,0:T(8,128)(2,1)S(1)} %shard_map.113.kv0_ref), channel_id=1, source_target_pairs={{0,2},{1,3},{4,6},{5,7},{8,10},{9,11},{12,14},{13,15},{16,18},{17,... | collective-permute-start | bytes 1572872 | tf_op jit(solution)/shard_map/ppermute | solution.py:78
  138.1 6.3 %collective-permute-done.kv1_ref = bf16[256,1024]{1,0:T(8,128)(2,1)S(1)} collective-permute-done((bf16[256,1024]{1,0:T(8,128)(2,1)S(1)}, bf16[256,1024]{1,0:T(8,128)(2,1)S(1)}, u32[]{:S(2)}, u32[]{:S(2)}) %collective-permute-start) | collective-permute-done | bytes 524320 | tf_op jit(solution)/shard_map/ppermute | solution.py:78
  144.3 11.3 %collective-permute-done.1.kv2_ref = bf16[256,1024]{1,0:T(8,128)(2,1)S(1)} collective-permute-done((bf16[256,1024]{1,0:T(8,128)(2,1)S(1)}, bf16[256,1024]{1,0:T(8,128)(2,1)S(1)}, u32[]{:S(2)}, u32[]{:S(2)}) %collective-permute-start.1) | collective-permute-done | bytes 524320 | tf_op jit(solution)/shard_map/ppermute | solution.py:78
  155.6 0.0 copy-start.6
  155.6 1.0 copy-done.6
  156.6 0.0 copy-start.9
  156.6 1.0 copy-done.9
  157.6 0.0 copy-start.16
  157.6 1.6 copy-done.16
  159.2 11.2 %shard_map.115 = bf16[256,4096]{1,0:T(8,128)(2,1)} custom-call(bf16[256,4096]{1,0:T(8,128)(2,1)S(1)} %bitcast.19, bf16[256,1024]{1,0:T(8,128)(2,1)S(1)} %shard_map.113.kv0_ref, bf16[256,1024]{1,0:T(8,128)(2,1)S(1)} %collective-permute-done.kv1_ref, bf16[256,1024]{1,0:T(8,128)(2,1)S(1)} %collective-permute-done.1.kv2_ref, ...), custom_call_target="tpu_custom_call" | custom-call | flops 3221225472 | bytes 5767168 | tf_op jit(solution)/shard_map/pallas_call | solution.py:183
  170.4 7.3 %all-to-all-done.2 = bf16[64,16,1024]{2,1,0:T(8,128)(2,1)S(1)} async-done(((bf16[64,16,1024]{2,1,0:T(8,128)(2,1)}), bf16[64,16,1024]{2,1,0:T(8,128)(2,1)S(1)}, u32[]{:S(2)}, u32[]{:S(2)}) %all-to-all-start.2) | async-done | bytes 2097184 | tf_op jit(solution)/shard_map/all_to_all | solution.py:245
  177.7 2.1 %shard_map.119 = bf16[16,16,4096]{2,1,0:T(8,128)(2,1)} custom-call(bf16[16,4,16,1024]{3,2,1,0:T(8,128)(2,1)S(1)} %bitcast.11), custom_call_target="tpu_custom_call" | custom-call | tf_op jit(solution)/shard_map/pallas_call | solution.py:233
Async XLA Ops:
  0.6 1.0 copy-start.10
  1.6 0.9 copy-start.11
  2.5 0.7 copy-start.14
  3.3 0.7 copy-start.17
  4.1 8.6 %collective-permute-start.2 = (bf16[272,384]{1,0:T(8,128)(2,1)S(1)}, bf16[272,384]{1,0:T(8,128)(2,1)S(1)}, u32[]{:S(2)}, u32[]{:S(2)}) collective-permute-start(bf16[272,384]{1,0:T(8,128)(2,1)S(1)} %get-tuple-element.4.down0_ref.along0_ref.kv0_ref), channel_id=1, source_target_pairs={{0,1},{1,2},{2,3},{4,5},{5,6},{6,7},{8,9},{9,10},{10,11},{12,13},{... | collective-permute-start | bytes 626696 | tf_op jit(solution)/shard_map/ppermute | solution.py:78
  8.1 8.0 %collective-permute-start.3 = (bf16[272,384]{1,0:T(8,128)(2,1)S(1)}, bf16[272,384]{1,0:T(8,128)(2,1)S(1)}, u32[]{:S(2)}, u32[]{:S(2)}) collective-permute-start(bf16[272,384]{1,0:T(8,128)(2,1)S(1)} %get-tuple-element.4.down0_ref.along0_ref.kv0_ref), channel_id=1, source_target_pairs={{0,2},{1,3},{4,6},{5,7},{8,10},{9,11},{12,14},{13,15},{16,18},{17,... | collective-permute-start | bytes 626696 | tf_op jit(solution)/shard_map/ppermute | solution.py:78
  16.1 1.6 copy-start.1
  17.7 1.0 copy-start.4
  18.7 1.0 copy-start.7
  19.7 35.4 %copy-start.2 = (bf16[1,256,4096]{2,1,0:T(8,128)(2,1)S(1)}, bf16[1,256,4096]{2,1,0:T(8,128)(2,1)}, u32[]{:S(2)}) copy-start(bf16[1,256,4096]{2,1,0:T(8,128)(2,1)} %param.13) | copy-start | bytes 6291460
  23.4 43.9 %all-to-all-start = ((bf16[64,16,256]{2,1,0:T(8,128)(2,1)}), bf16[64,16,256]{2,1,0:T(8,128)(2,1)S(1)}, u32[]{:S(2)}, u32[]{:S(2)}) async-start(bf16[64,16,256]{2,1,0:T(8,128)(2,1)} %bitcast.7), calls=%async_computation | async-start | bytes 1048576 | tf_op jit(solution)/shard_map/all_to_all | solution.py:245
  36.7 9.9 %collective-permute-start.4 = (bf16[256,768]{1,0:T(8,128)(2,1)}, bf16[256,768]{1,0:T(8,128)(2,1)S(1)}, u32[]{:S(2)}, u32[]{:S(2)}) collective-permute-start(bf16[256,768]{1,0:T(8,128)(2,1)} %copy-done.17), channel_id=1, source_target_pairs={{0,1},{1,2},{2,3},{4,5},{5,6},{6,7},{8,9},{9,10},{10,11},{12,13},{... | collective-permute-start | bytes 1179656 | tf_op jit(solution)/shard_map/ppermute | solution.py:78
  38.1 17.1 %collective-permute-start.5 = (bf16[256,768]{1,0:T(8,128)(2,1)}, bf16[256,768]{1,0:T(8,128)(2,1)S(1)}, u32[]{:S(2)}, u32[]{:S(2)}) collective-permute-start(bf16[256,768]{1,0:T(8,128)(2,1)} %copy-done.17), channel_id=1, source_target_pairs={{0,2},{1,3},{4,6},{5,7},{8,10},{9,11},{12,14},{13,15},{16,18},{17,... | collective-permute-start | bytes 1179656 | tf_op jit(solution)/shard_map/ppermute | solution.py:78
  55.2 1.0 copy-start.5
  56.2 1.0 copy-start.8
  57.1 1.0 copy-start.18
  66.1 1.1 copy-start.3
  67.3 50.9 %copy-start.15 = (s32[64]{0:T(128)S(1)}, s32[64]{0:T(128)}, u32[]{:S(2)}) copy-start(s32[64]{0:T(128)} %plan_ref.1) | copy-start | bytes 772
  118.9 1.3 copy-start
  120.2 6.3 %copy-start.12 = (bf16[1,256,512]{2,1,0:T(8,128)(2,1)S(1)}, bf16[1,256,512]{2,1,0:T(8,128)(2,1)}, u32[]{:S(2)}) copy-start(bf16[1,256,512]{2,1,0:T(8,128)(2,1)} %param.11) | copy-start | bytes 786436
  120.2 57.5 %all-to-all-start.2 = ((bf16[64,16,1024]{2,1,0:T(8,128)(2,1)}), bf16[64,16,1024]{2,1,0:T(8,128)(2,1)S(1)}, u32[]{:S(2)}, u32[]{:S(2)}) async-start(bf16[64,16,1024]{2,1,0:T(8,128)(2,1)} %copy-done), calls=%async_computation.2 | async-start | bytes 4194304 | tf_op jit(solution)/shard_map/all_to_all | solution.py:245
  126.5 1.0 copy-start.13
  127.6 16.8 %collective-permute-start = (bf16[256,1024]{1,0:T(8,128)(2,1)S(1)}, bf16[256,1024]{1,0:T(8,128)(2,1)S(1)}, u32[]{:S(2)}, u32[]{:S(2)}) collective-permute-start(bf16[256,1024]{1,0:T(8,128)(2,1)S(1)} %shard_map.113.kv0_ref), channel_id=1, source_target_pairs={{0,1},{1,2},{2,3},{4,5},{5,6},{6,7},{8,9},{9,10},{10,11},{12,13},{... | collective-permute-start | bytes 1572872 | tf_op jit(solution)/shard_map/ppermute | solution.py:78
  133.5 22.1 %collective-permute-start.1 = (bf16[256,1024]{1,0:T(8,128)(2,1)S(1)}, bf16[256,1024]{1,0:T(8,128)(2,1)S(1)}, u32[]{:S(2)}, u32[]{:S(2)}) collective-permute-start(bf16[256,1024]{1,0:T(8,128)(2,1)S(1)} %shard_map.113.kv0_ref), channel_id=1, source_target_pairs={{0,2},{1,3},{4,6},{5,7},{8,10},{9,11},{12,14},{13,15},{16,18},{17,... | collective-permute-start | bytes 1572872 | tf_op jit(solution)/shard_map/ppermute | solution.py:78
  155.6 1.0 copy-start.6
  156.6 1.0 copy-start.9
  157.6 1.6 copy-start.16
where the time goes:
time: 183 us; the launch traced here: 180 us
  blocking collectives  50.9 us (28%)
  starting transfers between devices  46.2 us (25%)
  waiting for transfers between devices  39.1 us (21%)
  Pallas kernels  25.9 us (14%)
  local copies, waits for them, and re-layouts  16.9 us (9%)
    all_to_all x1, blocking collectives, swap(): return lax.all_to_all(x, 'dp', split_axis=0, concat_axis=0, tiled=True)  50.9 us
    ppermute x6, waiting for transfers between devices, from_previous(): return lax.ppermute(x, 'sp', [(i, i + step) for i in range(size - step)])  31.8 us
    ppermute x6, starting transfers between devices, from_previous(): return lax.ppermute(x, 'sp', [(i, i + step) for i in range(size - step)])  26.6 us
    pallas_call x3, Pallas kernels, attend(): pl.pallas_call(functools.partial(attend_kernel, pieces), grid=(count,), i...  22.8 us
    all_to_all x2, starting transfers between devices, swap(): return lax.all_to_all(x, 'dp', split_axis=0, concat_axis=0, tiled=True)  19.6 us
    unnamed x38, local copies, waits for them, and re-layouts  16.9 us
    all_to_all x2, waiting for transfers between devices, swap(): return lax.all_to_all(x, 'dp', split_axis=0, concat_axis=0, tiled=True)  7.31 us
  transfers between devices with their start and end apart: 8, of which 6 were waited for; matrix products, arithmetic and copies ran while one was open for 0% of the time, Pallas kernels for 11%

commit v1 on v0

--- a/solution.py
+++ b/solution.py
@@ -22,6 +22,11 @@
 MASKED = -1e30
 BF = jnp.bfloat16
 F32 = jnp.float32
+SMALL = pltpu.CompilerParams(vmem_limit_bytes=16 << 20)
+
+
+def in_hbm(x):
+    return pltpu.with_memory_space_constraint(x, pltpu.HBM)
 
 
 def angle_tables():
@@ -31,51 +36,46 @@
     return np.cos(angle).astype(np.float32), np.sin(angle).astype(np.float32)
 
 
-def pack_first_kernel(k_ref, v_ref, lab_ref, first_ref, rest_ref):
+def pack_lead_kernel(k_ref, v_ref, lab_ref, out_ref):
     width = LEAD * 256
-    for c in range(KEY_VALUE_HEADS):
-        k = k_ref[:, c * 128 : (c + 1) * 128]
-        v = v_ref[:, c * 128 : (c + 1) * 128]
-        if c < LEAD:
-            first_ref[0:ROWS, c * 256 : c * 256 + 128] = k
-            first_ref[0:ROWS, c * 256 + 128 : c * 256 + 256] = v
-        else:
-            rest_ref[:, (c - LEAD) * 256 : (c - LEAD) * 256 + 128] = k
-            rest_ref[:, (c - LEAD) * 256 + 128 : (c - LEAD) * 256 + 256] = v
+    for c in range(LEAD):
+        out_ref[0:ROWS, c * 256 : c * 256 + 128] = k_ref[:, c * 128 : (c + 1) * 128]
+        out_ref[0:ROWS, c * 256 + 128 : c * 256 + 256] = v_ref[:, c * 128 : (c + 1) * 128]
     along = (lab_ref[...] + 1).astype(F32)
     down = jnp.transpose(jnp.broadcast_to(along, (128, ROWS)))
-    first_ref[0:ROWS, width : width + 128] = down.astype(BF)
-    first_ref[ROWS : ROWS + 16, :] = jnp.zeros((16, width + 128), BF)
-    first_ref[ROWS : ROWS + 16, 0:ROWS] = jnp.broadcast_to(along, (16, ROWS)).astype(BF)
-
-
-def pack_first(k, v, labels):
-    return pl.pallas_call(
-        pack_first_kernel,
-        out_shape=(
-            jax.ShapeDtypeStruct((ROWS + 16, LEAD * 256 + 128), BF),
-            jax.ShapeDtypeStruct((ROWS, (KEY_VALUE_HEADS - LEAD) * 256), BF),
-        ),
-        compiler_params=pltpu.CompilerParams(vmem_limit_bytes=16 << 20),
-    )(k, v, labels)
-
-
-def pack_plain_kernel(k_ref, v_ref, out_ref):
-    for c in range(KEY_VALUE_HEADS):
-        out_ref[:, c * 256 : c * 256 + 128] = k_ref[:, c * 128 : (c + 1) * 128]
-        out_ref[:, c * 256 + 128 : c * 256 + 256] = v_ref[:, c * 128 : (c + 1) * 128]
-
-
-def pack_plain(k, v):
-    return pl.pallas_call(
-        pack_plain_kernel,
-        out_shape=jax.ShapeDtypeStruct((ROWS, KEY_VALUE_HEADS * 256), BF),
-        compiler_params=pltpu.CompilerParams(vmem_limit_bytes=16 << 20),
-    )(k, v)
+    out_ref[0:ROWS, width : width + 128] = down.astype(BF)
+    out_ref[ROWS : ROWS + 16, ROWS:] = jnp.zeros((16, width + 128 - ROWS), BF)
+    out_ref[ROWS : ROWS + 16, 0:ROWS] = jnp.broadcast_to(along, (16, ROWS)).astype(BF)
+
+
+def pack_lead(k, v, labels):
+    half = pl.BlockSpec((ROWS, LEAD * 128), lambda i: (0, 0))
+    return pl.pallas_call(
+        pack_lead_kernel,
+        grid=(1,),
+        in_specs=[half, half, pl.BlockSpec((1, ROWS), lambda i: (0, 0))],
+        out_specs=pl.BlockSpec((ROWS + 16, LEAD * 256 + 128), lambda i: (0, 0)),
+        out_shape=jax.ShapeDtypeStruct((ROWS + 16, LEAD * 256 + 128), BF),
+        compiler_params=SMALL,
+    )(in_hbm(k), in_hbm(v), in_hbm(labels))
+
+
+def pack_kernel(first, k_ref, v_ref, out_ref):
+    for i, c in enumerate(range(first, KEY_VALUE_HEADS)):
+        out_ref[:, i * 256 : i * 256 + 128] = k_ref[:, c * 128 : (c + 1) * 128]
+        out_ref[:, i * 256 + 128 : i * 256 + 256] = v_ref[:, c * 128 : (c + 1) * 128]
+
+
+def pack(k, v, first):
+    return pl.pallas_call(
+        functools.partial(pack_kernel, first),
+        out_shape=jax.ShapeDtypeStruct((ROWS, (KEY_VALUE_HEADS - first) * 256), BF),
+        compiler_params=SMALL,
+    )(in_hbm(k), in_hbm(v))
 
 
 def from_previous(x, size, step):
-    return lax.ppermute(x, "sp", [(i, i + step) for i in range(size - step)])
+    return lax.ppermute(x, "sp", [(i, (i + step) % size) for i in range(size)])
 
 
 def rotate(x, cosine, sine):
@@ -85,6 +85,7 @@
 
 def attend_kernel(
     pieces,
+    place_ref,
     q_ref,
     kv0_ref,
     kv1_ref,
@@ -111,6 +112,9 @@
     def _():
         along = [ref[0:1, :].astype(F32) for ref in (along2_ref, along1_ref, along0_ref)]
         down = [ref[...].astype(F32) for ref in (down2_ref, down1_ref, down0_ref)]
+        back = [jnp.where(place_ref[0] >= n, 1.0, 0.0) for n in (2, 1)]
+        along = [along[0] * back[0], along[1] * back[1], along[2]]
+        down = [down[0] * back[0], down[1] * back[1], down[2]]
         place = lax.broadcasted_iota(jnp.int32, (1, ROWS), 1)
         starts = []
         for label in range(1, SEGS + 1):
@@ -167,15 +171,16 @@
             out_ref[:, h * 128 : (h + 1) * 128] = o
 
 
-def attend(pieces, q, first, count, kvs, lab, tables):
+def attend(pieces, q, first, count, kvs, lab, tables, weight=1):
     width = LEAD * 256
-    specs = [pl.BlockSpec((ROWS, GROUP * 128), lambda c: (0, c + first))]
+    specs = [pl.BlockSpec(memory_space=pltpu.SMEM)]
+    specs += [pl.BlockSpec((ROWS, GROUP * 128), lambda c: (0, c + first))]
     specs += [pl.BlockSpec((ROWS, 256), lambda c: (0, c))] * 3
     specs += [pl.BlockSpec((ROWS, 128), lambda c: (0, width // 128))] * 3
     specs += [pl.BlockSpec((16, ROWS), lambda c: (ROWS // 16, 0))] * 3
     specs += [pl.BlockSpec((3 * ROWS, HEAD_SIZE), lambda c: (0, 0))] * 2
     if pieces:
-        out_shape = jax.ShapeDtypeStruct((16, 4, 16, count * 256), BF)
+        out_shape = pltpu.HBM((16, 4, 16, count * 256), BF)
         out_spec = pl.BlockSpec((16, 4, 16, 256), lambda c: (0, 0, 0, c))
     else:
         out_shape = jax.ShapeDtypeStruct((ROWS, QUERY_HEADS * HEAD_SIZE), BF)
@@ -194,33 +199,43 @@
         ],
         compiler_params=pltpu.CompilerParams(vmem_limit_bytes=32 << 20),
         cost_estimate=pl.CostEstimate(
-            flops=count * GROUP * 4 * ROWS * 3 * ROWS * HEAD_SIZE,
+            flops=weight * count * GROUP * 4 * ROWS * 3 * ROWS * HEAD_SIZE,
             bytes_accessed=count * ROWS * (GROUP * 256 * 2 + 3 * 512),
             transcendentals=count * GROUP * ROWS * 2 * ROWS,
         ),
-    )(q, *kvs, *lab, *lab, *tables)
+    )(lax.axis_index("sp").astype(jnp.int32)[None], in_hbm(q), *kvs, *lab, *lab, *(in_hbm(t) for t in tables))
 
 
 def pick_kernel(plan_ref, lead_ref, rest_ref, out_ref):
-    width = LEAD * 256
-
-    def one(u, carry):
-        g = plan_ref[u]
-        out_ref[g, :, 0:width] = lead_ref[u]
-        out_ref[g, :, width:1024] = rest_ref[u]
-        return carry
-
-    lax.fori_loop(0, OWNERS, one, 0, unroll=8)
+    def place(ref):
+        def one(u, carry):
+            out_ref[plan_ref[u]] = ref[u]
+            return carry
+
+        lax.fori_loop(0, OWNERS, one, 0, unroll=16)
+
+    @pl.when(pl.program_id(0) < LEAD)
+    def _():
+        place(lead_ref)
+
+    @pl.when(pl.program_id(0) >= LEAD)
+    def _():
+        place(rest_ref)
 
 
 def pick(plan, lead, rest):
-    whole = pl.BlockSpec(memory_space=pltpu.VMEM)
+    block = (OWNERS, 16, 256)
     return pl.pallas_call(
         pick_kernel,
-        in_specs=[pl.BlockSpec(memory_space=pltpu.SMEM), whole, whole],
-        out_specs=whole,
-        out_shape=jax.ShapeDtypeStruct((OWNERS, 16, 1024), BF),
-        compiler_params=pltpu.CompilerParams(vmem_limit_bytes=16 << 20),
+        grid=(KEY_VALUE_HEADS,),
+        in_specs=[
+            pl.BlockSpec(memory_space=pltpu.SMEM),
+            pl.BlockSpec(block, lambda c: (0, 0, jnp.minimum(c, LEAD - 1))),
+            pl.BlockSpec(block, lambda c: (0, 0, jnp.maximum(c - LEAD, 0))),
+        ],
+        out_specs=pl.BlockSpec(block, lambda c: (0, 0, c)),
+        out_shape=pltpu.HBM((OWNERS, 16, 1024), BF),
+        compiler_params=SMALL,
     )(plan, lead, rest)
 
 
@@ -236,7 +251,7 @@
         in_specs=[pl.BlockSpec((16, 4, 16, 256), lambda c: (0, 0, 0, c))],
         out_specs=pl.BlockSpec((16, 16, 1024), lambda c: (0, 0, c)),
         out_shape=jax.ShapeDtypeStruct((16, 16, 4096), BF),
-        compiler_params=pltpu.CompilerParams(vmem_limit_bytes=16 << 20),
+        compiler_params=SMALL,
     )(arrived.reshape(16, 4, 16, 1024))
     return out.reshape(ROWS, 4096)
 
@@ -250,18 +265,20 @@
     bq, bk, bv, aq, ak, av = (t[0] for t in (bq, bk, bv, aq, ak, av))
     tables = tuple(jnp.asarray(t) for t in angle_tables())
 
-    head, rest = pack_first(ak, av, labels)
+    head = pack_lead(ak, av, labels)
     head1, head2 = (from_previous(head, size, s) for s in (1, 2))
     lab = (head, head1, head2)
     lead = attend(True, aq, 0, LEAD, lab, lab, tables)
     lead = swap(lead.reshape(OWNERS, 16, LEAD * 256))
 
+    rest = pack(ak, av, LEAD)
+    rest, _, _ = lax.optimization_barrier((rest, head1, head2))
     rest1, rest2 = (from_previous(rest, size, s) for s in (1, 2))
     others = KEY_VALUE_HEADS - LEAD
-    other = attend(True, aq, LEAD, others, (rest, rest1, rest2), lab, tables)
+    other = attend(True, aq, LEAD, others, (rest, rest1, rest2), lab, tables, 30)
     other = swap(other.reshape(OWNERS, 16, others * 256))
 
-    base = pack_plain(bk, bv)
+    base = pack(bk, bv, 0)
     base1, base2 = (from_previous(base, size, s) for s in (1, 2))
     base_output = attend(False, bq, 0, KEY_VALUE_HEADS, (base, base1, base2), lab, tables)
 

time: 183 us -> 161 us (0.88); the launches traced: 180 us -> 160 us
  starting transfers between devices: 46.2 us -> 28.2 us
  local copies, waits for them, and re-layouts: 16.9 us -> 0.01 us
  waiting for transfers between devices: 39.1 us -> 50 us
  Pallas kernels: 25.9 us -> 34.7 us
  blocking collectives: 50.9 us -> 46.3 us
    ppermute x6, starting transfers between devices: 26.6 us -> 8.55 us  [from_previous(): return lax.ppermute(x, 'sp', [(i, (i + step) % size) for i in range(size)])]
    unnamed x38 -> x2, local copies, waits for them, and re-layouts: 16.9 us -> 0.01 us
    all_to_all x2, waiting for transfers between devices: 7.31 us -> 19.1 us  [swap(): return lax.all_to_all(x, 'dp', split_axis=0, concat_axis=0, tiled=True)]
    pallas_call x3 -> x4, Pallas kernels: 0.99 us -> 5.85 us  [the longest x1 2.59 us: pick(): pl.pallas_call(pick_kernel, grid=(KEY_VALUE_HEADS,), in_specs=[pl.BlockSp...]
    all_to_all x1, blocking collectives: 50.9 us -> 46.3 us  [swap(): return lax.all_to_all(x, 'dp', split_axis=0, concat_axis=0, tiled=True)]
    pallas_call x3, Pallas kernels: 22.8 us -> 26.7 us  [attend(): pl.pallas_call(functools.partial(attend_kernel, pieces), grid=(count,), i...]
  transfers between devices with their start and end apart: 8 -> 8, of which waited for: 6 -> 7; matrix products, arithmetic and copies ran while one was open for 0% -> 0% of each run, Pallas kernels for 11% -> 18%
where the time goes in v1:
time: 161 us; the launch traced here: 160 us
  waiting for transfers between devices  50 us (31%)
  blocking collectives  46.3 us (29%)
  Pallas kernels  34.7 us (22%)
  starting transfers between devices  28.2 us (18%)
    all_to_all x1, blocking collectives, swap(): return lax.all_to_all(x, 'dp', split_axis=0, concat_axis=0, tiled=True)  46.3 us
    ppermute x6, waiting for transfers between devices, from_previous(): return lax.ppermute(x, 'sp', [(i, (i + step) % size) for i in range(size)])  30.8 us
    pallas_call x3, Pallas kernels, attend(): pl.pallas_call(functools.partial(attend_kernel, pieces), grid=(count,), i...  26.7 us
    all_to_all x2, starting transfers between devices, swap(): return lax.all_to_all(x, 'dp', split_axis=0, concat_axis=0, tiled=True)  19.7 us
    all_to_all x2, waiting for transfers between devices, swap(): return lax.all_to_all(x, 'dp', split_axis=0, concat_axis=0, tiled=True)  19.1 us
    ppermute x6, starting transfers between devices, from_previous(): return lax.ppermute(x, 'sp', [(i, (i + step) % size) for i in range(size)])  8.55 us
  transfers between devices with their start and end apart: 8, of which 7 were waited for; matrix products, arithmetic and copies ran while one was open for 0% of the time, Pallas kernels for 18%

profile of v1, /device:TPU:1, one launch (start us, length us, event | category | flops | bytes accessed | tf_op | source)
XLA Modules:
  0.0 159.9 jit_solution(14004765356656721254)
XLA Ops:
  0.6 1.0 shard_map.114.down0_ref.along0_ref.kv0_ref
  1.6 2.2 %collective-permute-start.2 = (bf16[272,384]{1,0:T(8,128)(2,1)S(1)}, bf16[272,384]{1,0:T(8,128)(2,1)S(1)}, u32[]{:S(2)}, u32[]{:S(2)}) collective-permute-start(bf16[272,384]{1,0:T(8,128)(2,1)S(1)} %shard_map.114.down0_ref.along0_ref.kv0_ref), channel_id=1, source_target_pairs={{0,1},{1,2},{2,3},{3,0},{4,5},{5,6},{6,7},{7,4},{8,9},{9,10},{10,1... | collective-permute-start | bytes 626696 | tf_op jit(solution)/shard_map/ppermute | solution.py:78
  3.8 2.6 %collective-permute-start.3 = (bf16[272,384]{1,0:T(8,128)(2,1)S(1)}, bf16[272,384]{1,0:T(8,128)(2,1)S(1)}, u32[]{:S(2)}, u32[]{:S(2)}) collective-permute-start(bf16[272,384]{1,0:T(8,128)(2,1)S(1)} %shard_map.114.down0_ref.along0_ref.kv0_ref), channel_id=1, source_target_pairs={{0,2},{1,3},{2,0},{3,1},{4,6},{5,7},{6,4},{7,5},{8,10},{9,11},{10,... | collective-permute-start | bytes 626696 | tf_op jit(solution)/shard_map/ppermute | solution.py:78
  6.5 1.1 shard_map.117.kv0_ref
  7.6 0.9 collective-permute-done.2.down1_ref.along1_ref.kv1_ref
  8.5 7.0 %collective-permute-done.3.down2_ref.along2_ref.kv2_ref = bf16[272,384]{1,0:T(8,128)(2,1)S(1)} collective-permute-done((bf16[272,384]{1,0:T(8,128)(2,1)S(1)}, bf16[272,384]{1,0:T(8,128)(2,1)S(1)}, u32[]{:S(2)}, u32[]{:S(2)}) %collective-permute-start.3) | collective-permute-done | bytes 208928 | tf_op jit(solution)/shard_map/ppermute | solution.py:78
  15.5 0.0 collective-permute-start.4
  15.5 0.2 collective-permute-start.5
  15.7 4.9 %shard_map.116 = bf16[16,4,16,256]{3,2,1,0:T(8,128)(2,1)} custom-call(s32[1]{0:T(128)} %bitcast.place_ref, bf16[256,4096]{1,0:T(8,128)(2,1)} %bitcast.13, bf16[272,384]{1,0:T(8,128)(2,1)S(1)} %shard_map.114.down0_ref.along0_ref.kv0_ref, bf16[272,384]{1,0:T(8,128)(2,1)S(1)} %collective-permute-done.2.down1_ref.along1_ref.kv1_ref, ...), custom_call_target="tpu_custom_call" | custom-call | flops 805306368 | bytes 1441792 | tf_op jit(solution)/shard_map/pallas_call | solution.py:188
  20.6 13.6 %all-to-all-start = ((bf16[64,16,256]{2,1,0:T(8,128)(2,1)}), bf16[64,16,256]{2,1,0:T(8,128)(2,1)S(1)}, u32[]{:S(2)}, u32[]{:S(2)}) async-start(bf16[64,16,256]{2,1,0:T(8,128)(2,1)} %bitcast.15), calls=%async_computation | async-start | bytes 1048576 | tf_op jit(solution)/shard_map/all_to_all | solution.py:260
  34.1 0.1 collective-permute-done.4.kv1_ref
  34.2 0.0 collective-permute-done.5.kv2_ref
  34.2 9.7 %shard_map.118 = bf16[16,4,16,768]{3,2,1,0:T(8,128)(2,1)} custom-call(s32[1]{0:T(128)} %bitcast.place_ref, bf16[256,4096]{1,0:T(8,128)(2,1)} %bitcast.14, bf16[256,768]{1,0:T(8,128)(2,1)S(1)} %shard_map.117.kv0_ref, bf16[256,768]{1,0:T(8,128)(2,1)S(1)} %collective-permute-done.4.kv1_ref, bf16[256,768]{1,0:T(8,128)(2,1)S(1)} %collective-permute-done.5.kv2_ref, ...), custom_call_target="tpu_custom_call" | custom-call | flops 72477573120 | bytes 4325376 | tf_op jit(solution)/shard_map/pallas_call | solution.py:188
  43.9 0.0 copy-start
  43.9 7.5 %all-to-all-done.lead_ref = bf16[64,16,256]{2,1,0:T(8,128)(2,1)S(1)} async-done(((bf16[64,16,256]{2,1,0:T(8,128)(2,1)}), bf16[64,16,256]{2,1,0:T(8,128)(2,1)S(1)}, u32[]{:S(2)}, u32[]{:S(2)}) %all-to-all-start) | async-done | bytes 524320 | tf_op jit(solution)/shard_map/all_to_all | solution.py:260
  51.5 46.3 %all_to_all.15.rest_ref = bf16[64,16,768]{2,1,0:T(8,128)(2,1)S(1)} all-to-all(bf16[64,16,768]{2,1,0:T(8,128)(2,1)} %bitcast.17), channel_id=1, replica_groups=mesh['dp'=64,'sp'=4] {'dp'}, dimensions={0} | all-to-all | bytes 3145728 | tf_op jit(solution)/shard_map/all_to_all | solution.py:260
  97.8 0.0 copy-done
  97.8 2.6 %shard_map.119 = bf16[64,16,1024]{2,1,0:T(8,128)(2,1)} custom-call(s32[64]{0:T(128)S(1)} %copy-done, bf16[64,16,256]{2,1,0:T(8,128)(2,1)S(1)} %all-to-all-done.lead_ref, bf16[64,16,768]{2,1,0:T(8,128)(2,1)S(1)} %all_to_all.15.rest_ref), custom_call_target="tpu_custom_call" | custom-call | tf_op jit(solution)/shard_map/pallas_call | solution.py:228
  100.4 6.1 %all-to-all-start.2 = ((bf16[64,16,1024]{2,1,0:T(8,128)(2,1)}), bf16[64,16,1024]{2,1,0:T(8,128)(2,1)S(1)}, u32[]{:S(2)}, u32[]{:S(2)}) async-start(bf16[64,16,1024]{2,1,0:T(8,128)(2,1)} %shard_map.119), calls=%async_computation.2 | async-start | bytes 4194304 | tf_op jit(solution)/shard_map/all_to_all | solution.py:260
  106.5 1.2 shard_map.113.kv0_ref
  107.7 3.1 %collective-permute-start = (bf16[256,1024]{1,0:T(8,128)(2,1)S(1)}, bf16[256,1024]{1,0:T(8,128)(2,1)S(1)}, u32[]{:S(2)}, u32[]{:S(2)}) collective-permute-start(bf16[256,1024]{1,0:T(8,128)(2,1)S(1)} %shard_map.113.kv0_ref), channel_id=1, source_target_pairs={{0,1},{1,2},{2,3},{3,0},{4,5},{5,6},{6,7},{7,4},{8,9},{9,10},{10,1... | collective-permute-start | bytes 1572872 | tf_op jit(solution)/shard_map/ppermute | solution.py:78
  110.8 0.5 collective-permute-start.1
  111.2 11.0 %collective-permute-done.kv1_ref = bf16[256,1024]{1,0:T(8,128)(2,1)S(1)} collective-permute-done((bf16[256,1024]{1,0:T(8,128)(2,1)S(1)}, bf16[256,1024]{1,0:T(8,128)(2,1)S(1)}, u32[]{:S(2)}, u32[]{:S(2)}) %collective-permute-start) | collective-permute-done | bytes 524320 | tf_op jit(solution)/shard_map/ppermute | solution.py:78
  122.2 11.8 %collective-permute-done.1.kv2_ref = bf16[256,1024]{1,0:T(8,128)(2,1)S(1)} collective-permute-done((bf16[256,1024]{1,0:T(8,128)(2,1)S(1)}, bf16[256,1024]{1,0:T(8,128)(2,1)S(1)}, u32[]{:S(2)}, u32[]{:S(2)}) %collective-permute-start.1) | collective-permute-done | bytes 524320 | tf_op jit(solution)/shard_map/ppermute | solution.py:78
  134.0 12.1 %shard_map.115 = bf16[256,4096]{1,0:T(8,128)(2,1)} custom-call(s32[1]{0:T(128)} %bitcast.place_ref, bf16[256,4096]{1,0:T(8,128)(2,1)} %bitcast.24, bf16[256,1024]{1,0:T(8,128)(2,1)S(1)} %shard_map.113.kv0_ref, bf16[256,1024]{1,0:T(8,128)(2,1)S(1)} %collective-permute-done.kv1_ref, bf16[256,1024]{1,0:T(8,128)(2,1)S(1)} %collective-permute-done.1.kv2_ref, ...), custom_call_target="tpu_custom_call" | custom-call | flops 3221225472 | bytes 5767168 | tf_op jit(solution)/shard_map/pallas_call | solution.py:188
  146.2 11.6 %all-to-all-done.2 = bf16[64,16,1024]{2,1,0:T(8,128)(2,1)S(1)} async-done(((bf16[64,16,1024]{2,1,0:T(8,128)(2,1)}), bf16[64,16,1024]{2,1,0:T(8,128)(2,1)S(1)}, u32[]{:S(2)}, u32[]{:S(2)}) %all-to-all-start.2) | async-done | bytes 2097184 | tf_op jit(solution)/shard_map/all_to_all | solution.py:260
  157.8 2.1 %shard_map.120 = bf16[16,16,4096]{2,1,0:T(8,128)(2,1)} custom-call(bf16[16,4,16,1024]{3,2,1,0:T(8,128)(2,1)S(1)} %bitcast.12), custom_call_target="tpu_custom_call" | custom-call | tf_op jit(solution)/shard_map/pallas_call | solution.py:248
Async XLA Ops:
  1.6 6.8 %collective-permute-start.2 = (bf16[272,384]{1,0:T(8,128)(2,1)S(1)}, bf16[272,384]{1,0:T(8,128)(2,1)S(1)}, u32[]{:S(2)}, u32[]{:S(2)}) collective-permute-start(bf16[272,384]{1,0:T(8,128)(2,1)S(1)} %shard_map.114.down0_ref.along0_ref.kv0_ref), channel_id=1, source_target_pairs={{0,1},{1,2},{2,3},{3,0},{4,5},{5,6},{6,7},{7,4},{8,9},{9,10},{10,1... | collective-permute-start | bytes 626696 | tf_op jit(solution)/shard_map/ppermute | solution.py:78
  3.8 11.7 %collective-permute-start.3 = (bf16[272,384]{1,0:T(8,128)(2,1)S(1)}, bf16[272,384]{1,0:T(8,128)(2,1)S(1)}, u32[]{:S(2)}, u32[]{:S(2)}) collective-permute-start(bf16[272,384]{1,0:T(8,128)(2,1)S(1)} %shard_map.114.down0_ref.along0_ref.kv0_ref), channel_id=1, source_target_pairs={{0,2},{1,3},{2,0},{3,1},{4,6},{5,7},{6,4},{7,5},{8,10},{9,11},{10,... | collective-permute-start | bytes 626696 | tf_op jit(solution)/shard_map/ppermute | solution.py:78
  15.5 18.7 %collective-permute-start.4 = (bf16[256,768]{1,0:T(8,128)(2,1)S(1)}, bf16[256,768]{1,0:T(8,128)(2,1)S(1)}, u32[]{:S(2)}, u32[]{:S(2)}) collective-permute-start(bf16[256,768]{1,0:T(8,128)(2,1)S(1)} %shard_map.117.kv0_ref), channel_id=1, source_target_pairs={{0,1},{1,2},{2,3},{3,0},{4,5},{5,6},{6,7},{7,4},{8,9},{9,10},{10,1... | collective-permute-start | bytes 1179656 | tf_op jit(solution)/shard_map/ppermute | solution.py:78
  15.5 18.7 %collective-permute-start.5 = (bf16[256,768]{1,0:T(8,128)(2,1)S(1)}, bf16[256,768]{1,0:T(8,128)(2,1)S(1)}, u32[]{:S(2)}, u32[]{:S(2)}) collective-permute-start(bf16[256,768]{1,0:T(8,128)(2,1)S(1)} %shard_map.117.kv0_ref), channel_id=1, source_target_pairs={{0,2},{1,3},{2,0},{3,1},{4,6},{5,7},{6,4},{7,5},{8,10},{9,11},{10,... | collective-permute-start | bytes 1179656 | tf_op jit(solution)/shard_map/ppermute | solution.py:78
  20.6 30.9 %all-to-all-start = ((bf16[64,16,256]{2,1,0:T(8,128)(2,1)}), bf16[64,16,256]{2,1,0:T(8,128)(2,1)S(1)}, u32[]{:S(2)}, u32[]{:S(2)}) async-start(bf16[64,16,256]{2,1,0:T(8,128)(2,1)} %bitcast.15), calls=%async_computation | async-start | bytes 1048576 | tf_op jit(solution)/shard_map/all_to_all | solution.py:260
  43.9 53.9 %copy-start = (s32[64]{0:T(128)S(1)}, s32[64]{0:T(128)}, u32[]{:S(2)}) copy-start(s32[64]{0:T(128)} %plan_ref.1) | copy-start | bytes 772
  100.4 57.4 %all-to-all-start.2 = ((bf16[64,16,1024]{2,1,0:T(8,128)(2,1)}), bf16[64,16,1024]{2,1,0:T(8,128)(2,1)S(1)}, u32[]{:S(2)}, u32[]{:S(2)}) async-start(bf16[64,16,1024]{2,1,0:T(8,128)(2,1)} %shard_map.119), calls=%async_computation.2 | async-start | bytes 4194304 | tf_op jit(solution)/shard_map/all_to_all | solution.py:260
  107.7 14.5 %collective-permute-start = (bf16[256,1024]{1,0:T(8,128)(2,1)S(1)}, bf16[256,1024]{1,0:T(8,128)(2,1)S(1)}, u32[]{:S(2)}, u32[]{:S(2)}) collective-permute-start(bf16[256,1024]{1,0:T(8,128)(2,1)S(1)} %shard_map.113.kv0_ref), channel_id=1, source_target_pairs={{0,1},{1,2},{2,3},{3,0},{4,5},{5,6},{6,7},{7,4},{8,9},{9,10},{10,1... | collective-permute-start | bytes 1572872 | tf_op jit(solution)/shard_map/ppermute | solution.py:78
  110.8 23.3 %collective-permute-start.1 = (bf16[256,1024]{1,0:T(8,128)(2,1)S(1)}, bf16[256,1024]{1,0:T(8,128)(2,1)S(1)}, u32[]{:S(2)}, u32[]{:S(2)}) collective-permute-start(bf16[256,1024]{1,0:T(8,128)(2,1)S(1)} %shard_map.113.kv0_ref), channel_id=1, source_target_pairs={{0,2},{1,3},{2,0},{3,1},{4,6},{5,7},{6,4},{7,5},{8,10},{9,11},{10,... | collective-permute-start | bytes 1572872 | tf_op jit(solution)/shard_map/ppermute | solution.py:78

commit v2 on v1

--- a/solution.py
+++ b/solution.py
@@ -206,51 +206,72 @@
     )(lax.axis_index("sp").astype(jnp.int32)[None], in_hbm(q), *kvs, *lab, *lab, *(in_hbm(t) for t in tables))
 
 
-def pick_kernel(plan_ref, lead_ref, rest_ref, out_ref):
-    def place(ref):
-        def one(u, carry):
-            out_ref[plan_ref[u]] = ref[u]
+def pick_kernel(plan_ref, lead_ref, rest_ref, out_ref, source, stage, sems):
+    width = LEAD * 256
+    part = OWNERS // 4
+
+    def note(u, carry):
+        source[plan_ref[u]] = u
+        return carry
+
+    lax.fori_loop(0, OWNERS, note, 0, unroll=8)
+    copies = []
+    for p in range(4):
+        def one(i, carry, p=p):
+            u = source[p * part + i]
+            stage[p, i, :, 0:width] = lead_ref[u]
+            stage[p, i, :, width:] = rest_ref[u]
             return carry
 
-        lax.fori_loop(0, OWNERS, one, 0, unroll=16)
-
-    @pl.when(pl.program_id(0) < LEAD)
-    def _():
-        place(lead_ref)
-
-    @pl.when(pl.program_id(0) >= LEAD)
-    def _():
-        place(rest_ref)
+        lax.fori_loop(0, part, one, 0, unroll=4)
+        copies.append(
+            pltpu.make_async_copy(stage.at[p], out_ref.at[pl.ds(p * part, part)], sems.at[p])
+        )
+        copies[-1].start()
+    for copy in copies:
+        copy.wait()
 
 
 def pick(plan, lead, rest):
-    block = (OWNERS, 16, 256)
+    whole = pl.BlockSpec(memory_space=pltpu.VMEM)
     return pl.pallas_call(
         pick_kernel,
-        grid=(KEY_VALUE_HEADS,),
-        in_specs=[
-            pl.BlockSpec(memory_space=pltpu.SMEM),
-            pl.BlockSpec(block, lambda c: (0, 0, jnp.minimum(c, LEAD - 1))),
-            pl.BlockSpec(block, lambda c: (0, 0, jnp.maximum(c - LEAD, 0))),
+        in_specs=[pl.BlockSpec(memory_space=pltpu.SMEM), whole, whole],
+        out_specs=pl.BlockSpec(memory_space=pl.ANY),
+        out_shape=pltpu.HBM((OWNERS, 16, 1024), BF),
+        scratch_shapes=[
+            pltpu.SMEM((OWNERS,), jnp.int32),
+            pltpu.VMEM((4, OWNERS // 4, 16, 1024), BF),
+            pltpu.SemaphoreType.DMA((4,)),
         ],
-        out_specs=pl.BlockSpec(block, lambda c: (0, 0, c)),
-        out_shape=pltpu.HBM((OWNERS, 16, 1024), BF),
         compiler_params=SMALL,
     )(plan, lead, rest)
 
 
-def lay_kernel(in_ref, out_ref):
-    for cb in range(4):
-        out_ref[:, :, cb * 256 : (cb + 1) * 256] = in_ref[:, cb]
+def lay_kernel(in_ref, out_ref, sems):
+    copies = []
+    for c in range(KEY_VALUE_HEADS):
+        for cb in range(4):
+            copies.append(
+                pltpu.make_async_copy(
+                    in_ref.at[:, cb, :, pl.ds(c * 256, 256)],
+                    out_ref.at[:, :, pl.ds(c * 1024 + cb * 256, 256)],
+                    sems.at[c * 4 + cb],
+                )
+            )
+    for copy in copies:
+        copy.start()
+    for copy in copies:
+        copy.wait()
 
 
 def lay(arrived):
     out = pl.pallas_call(
         lay_kernel,
-        grid=(KEY_VALUE_HEADS,),
-        in_specs=[pl.BlockSpec((16, 4, 16, 256), lambda c: (0, 0, 0, c))],
-        out_specs=pl.BlockSpec((16, 16, 1024), lambda c: (0, 0, c)),
-        out_shape=jax.ShapeDtypeStruct((16, 16, 4096), BF),
+        in_specs=[pl.BlockSpec(memory_space=pltpu.VMEM)],
+        out_specs=pl.BlockSpec(memory_space=pl.ANY),
+        out_shape=pltpu.HBM((16, 16, 4096), BF),
+        scratch_shapes=[pltpu.SemaphoreType.DMA((16,))],
         compiler_params=SMALL,
     )(arrived.reshape(16, 4, 16, 1024))
     return out.reshape(ROWS, 4096)

time: 161 us -> 160 us (level)
  no operation moved by 1% of the time
where the time goes in v2:
time: 160 us; the launch traced here: 159 us
  waiting for transfers between devices  50 us (31%)
  blocking collectives  46.3 us (29%)
  Pallas kernels  33.5 us (21%)
  starting transfers between devices  28.3 us (18%)
    all_to_all x1, blocking collectives, swap(): return lax.all_to_all(x, 'dp', split_axis=0, concat_axis=0, tiled=True)  46.3 us
    ppermute x6, waiting for transfers between devices, from_previous(): return lax.ppermute(x, 'sp', [(i, (i + step) % size) for i in range(size)])  30.8 us
    pallas_call x3, Pallas kernels, attend(): pl.pallas_call(functools.partial(attend_kernel, pieces), grid=(count,), i...  26.7 us
    all_to_all x2, starting transfers between devices, swap(): return lax.all_to_all(x, 'dp', split_axis=0, concat_axis=0, tiled=True)  19.7 us
    all_to_all x2, waiting for transfers between devices, swap(): return lax.all_to_all(x, 'dp', split_axis=0, concat_axis=0, tiled=True)  19.1 us
    ppermute x6, starting transfers between devices, from_previous(): return lax.ppermute(x, 'sp', [(i, (i + step) % size) for i in range(size)])  8.55 us
  transfers between devices with their start and end apart: 8, of which 7 were waited for; matrix products, arithmetic and copies ran while one was open for 0% of the time, Pallas kernels for 18%

profile of v2, /device:TPU:1, one launch (start us, length us, event | category | flops | bytes accessed | tf_op | source)
XLA Modules:
  0.0 158.8 jit_solution(10242215444922172271)
XLA Ops:
  0.6 1.0 shard_map.114.down0_ref.along0_ref.kv0_ref
  1.6 2.2 %collective-permute-start.2 = (bf16[272,384]{1,0:T(8,128)(2,1)S(1)}, bf16[272,384]{1,0:T(8,128)(2,1)S(1)}, u32[]{:S(2)}, u32[]{:S(2)}) collective-permute-start(bf16[272,384]{1,0:T(8,128)(2,1)S(1)} %shard_map.114.down0_ref.along0_ref.kv0_ref), channel_id=1, source_target_pairs={{0,1},{1,2},{2,3},{3,0},{4,5},{5,6},{6,7},{7,4},{8,9},{9,10},{10,1... | collective-permute-start | bytes 626696 | tf_op jit(solution)/shard_map/ppermute | solution.py:78
  3.8 2.6 %collective-permute-start.3 = (bf16[272,384]{1,0:T(8,128)(2,1)S(1)}, bf16[272,384]{1,0:T(8,128)(2,1)S(1)}, u32[]{:S(2)}, u32[]{:S(2)}) collective-permute-start(bf16[272,384]{1,0:T(8,128)(2,1)S(1)} %shard_map.114.down0_ref.along0_ref.kv0_ref), channel_id=1, source_target_pairs={{0,2},{1,3},{2,0},{3,1},{4,6},{5,7},{6,4},{7,5},{8,10},{9,11},{10,... | collective-permute-start | bytes 626696 | tf_op jit(solution)/shard_map/ppermute | solution.py:78
  6.5 1.1 shard_map.117.kv0_ref
  7.6 0.9 collective-permute-done.2.down1_ref.along1_ref.kv1_ref
  8.5 7.0 %collective-permute-done.3.down2_ref.along2_ref.kv2_ref = bf16[272,384]{1,0:T(8,128)(2,1)S(1)} collective-permute-done((bf16[272,384]{1,0:T(8,128)(2,1)S(1)}, bf16[272,384]{1,0:T(8,128)(2,1)S(1)}, u32[]{:S(2)}, u32[]{:S(2)}) %collective-permute-start.3) | collective-permute-done | bytes 208928 | tf_op jit(solution)/shard_map/ppermute | solution.py:78
  15.5 0.0 collective-permute-start.4
  15.5 0.2 collective-permute-start.5
  15.7 4.9 %shard_map.116 = bf16[16,4,16,256]{3,2,1,0:T(8,128)(2,1)} custom-call(s32[1]{0:T(128)} %bitcast.place_ref, bf16[256,4096]{1,0:T(8,128)(2,1)} %bitcast.13, bf16[272,384]{1,0:T(8,128)(2,1)S(1)} %shard_map.114.down0_ref.along0_ref.kv0_ref, bf16[272,384]{1,0:T(8,128)(2,1)S(1)} %collective-permute-done.2.down1_ref.along1_ref.kv1_ref, ...), custom_call_target="tpu_custom_call" | custom-call | flops 805306368 | bytes 1441792 | tf_op jit(solution)/shard_map/pallas_call | solution.py:188
  20.6 13.6 %all-to-all-start = ((bf16[64,16,256]{2,1,0:T(8,128)(2,1)}), bf16[64,16,256]{2,1,0:T(8,128)(2,1)S(1)}, u32[]{:S(2)}, u32[]{:S(2)}) async-start(bf16[64,16,256]{2,1,0:T(8,128)(2,1)} %bitcast.15), calls=%async_computation | async-start | bytes 1048576 | tf_op jit(solution)/shard_map/all_to_all | solution.py:281
  34.1 0.1 collective-permute-done.4.kv1_ref
  34.2 0.0 collective-permute-done.5.kv2_ref
  34.2 9.7 %shard_map.118 = bf16[16,4,16,768]{3,2,1,0:T(8,128)(2,1)} custom-call(s32[1]{0:T(128)} %bitcast.place_ref, bf16[256,4096]{1,0:T(8,128)(2,1)} %bitcast.14, bf16[256,768]{1,0:T(8,128)(2,1)S(1)} %shard_map.117.kv0_ref, bf16[256,768]{1,0:T(8,128)(2,1)S(1)} %collective-permute-done.4.kv1_ref, bf16[256,768]{1,0:T(8,128)(2,1)S(1)} %collective-permute-done.5.kv2_ref, ...), custom_call_target="tpu_custom_call" | custom-call | flops 72477573120 | bytes 4325376 | tf_op jit(solution)/shard_map/pallas_call | solution.py:188
  43.9 0.0 copy-start
  43.9 7.5 %all-to-all-done.lead_ref = bf16[64,16,256]{2,1,0:T(8,128)(2,1)S(1)} async-done(((bf16[64,16,256]{2,1,0:T(8,128)(2,1)}), bf16[64,16,256]{2,1,0:T(8,128)(2,1)S(1)}, u32[]{:S(2)}, u32[]{:S(2)}) %all-to-all-start) | async-done | bytes 524320 | tf_op jit(solution)/shard_map/all_to_all | solution.py:281
  51.5 46.3 %all_to_all.15.rest_ref = bf16[64,16,768]{2,1,0:T(8,128)(2,1)S(1)} all-to-all(bf16[64,16,768]{2,1,0:T(8,128)(2,1)} %bitcast.17), channel_id=1, replica_groups=mesh['dp'=64,'sp'=4] {'dp'}, dimensions={0} | all-to-all | bytes 3145728 | tf_op jit(solution)/shard_map/all_to_all | solution.py:281
  97.8 0.0 copy-done
  97.8 2.0 %shard_map.119 = bf16[64,16,1024]{2,1,0:T(8,128)(2,1)} custom-call(s32[64]{0:T(128)S(1)} %copy-done, bf16[64,16,256]{2,1,0:T(8,128)(2,1)S(1)} %all-to-all-done.lead_ref, bf16[64,16,768]{2,1,0:T(8,128)(2,1)S(1)} %all_to_all.15.rest_ref), custom_call_target="tpu_custom_call" | custom-call | tf_op jit(solution)/shard_map/pallas_call | solution.py:237
  99.9 6.1 %all-to-all-start.2 = ((bf16[64,16,1024]{2,1,0:T(8,128)(2,1)}), bf16[64,16,1024]{2,1,0:T(8,128)(2,1)S(1)}, u32[]{:S(2)}, u32[]{:S(2)}) async-start(bf16[64,16,1024]{2,1,0:T(8,128)(2,1)} %shard_map.119), calls=%async_computation.2 | async-start | bytes 4194304 | tf_op jit(solution)/shard_map/all_to_all | solution.py:281
  106.0 1.2 shard_map.113.kv0_ref
  107.2 3.1 %collective-permute-start = (bf16[256,1024]{1,0:T(8,128)(2,1)S(1)}, bf16[256,1024]{1,0:T(8,128)(2,1)S(1)}, u32[]{:S(2)}, u32[]{:S(2)}) collective-permute-start(bf16[256,1024]{1,0:T(8,128)(2,1)S(1)} %shard_map.113.kv0_ref), channel_id=1, source_target_pairs={{0,1},{1,2},{2,3},{3,0},{4,5},{5,6},{6,7},{7,4},{8,9},{9,10},{10,1... | collective-permute-start | bytes 1572872 | tf_op jit(solution)/shard_map/ppermute | solution.py:78
  110.2 0.5 collective-permute-start.1
  110.7 11.0 %collective-permute-done.kv1_ref = bf16[256,1024]{1,0:T(8,128)(2,1)S(1)} collective-permute-done((bf16[256,1024]{1,0:T(8,128)(2,1)S(1)}, bf16[256,1024]{1,0:T(8,128)(2,1)S(1)}, u32[]{:S(2)}, u32[]{:S(2)}) %collective-permute-start) | collective-permute-done | bytes 524320 | tf_op jit(solution)/shard_map/ppermute | solution.py:78
  121.7 11.8 %collective-permute-done.1.kv2_ref = bf16[256,1024]{1,0:T(8,128)(2,1)S(1)} collective-permute-done((bf16[256,1024]{1,0:T(8,128)(2,1)S(1)}, bf16[256,1024]{1,0:T(8,128)(2,1)S(1)}, u32[]{:S(2)}, u32[]{:S(2)}) %collective-permute-start.1) | collective-permute-done | bytes 524320 | tf_op jit(solution)/shard_map/ppermute | solution.py:78
  133.5 12.1 %shard_map.115 = bf16[256,4096]{1,0:T(8,128)(2,1)} custom-call(s32[1]{0:T(128)} %bitcast.place_ref, bf16[256,4096]{1,0:T(8,128)(2,1)} %bitcast.24, bf16[256,1024]{1,0:T(8,128)(2,1)S(1)} %shard_map.113.kv0_ref, bf16[256,1024]{1,0:T(8,128)(2,1)S(1)} %collective-permute-done.kv1_ref, bf16[256,1024]{1,0:T(8,128)(2,1)S(1)} %collective-permute-done.1.kv2_ref, ...), custom_call_target="tpu_custom_call" | custom-call | flops 3221225472 | bytes 5767168 | tf_op jit(solution)/shard_map/pallas_call | solution.py:188
  145.6 11.6 %all-to-all-done.2 = bf16[64,16,1024]{2,1,0:T(8,128)(2,1)S(1)} async-done(((bf16[64,16,1024]{2,1,0:T(8,128)(2,1)}), bf16[64,16,1024]{2,1,0:T(8,128)(2,1)S(1)}, u32[]{:S(2)}, u32[]{:S(2)}) %all-to-all-start.2) | async-done | bytes 2097184 | tf_op jit(solution)/shard_map/all_to_all | solution.py:281
  157.2 1.4 shard_map.120
Async XLA Ops:
  1.6 6.8 %collective-permute-start.2 = (bf16[272,384]{1,0:T(8,128)(2,1)S(1)}, bf16[272,384]{1,0:T(8,128)(2,1)S(1)}, u32[]{:S(2)}, u32[]{:S(2)}) collective-permute-start(bf16[272,384]{1,0:T(8,128)(2,1)S(1)} %shard_map.114.down0_ref.along0_ref.kv0_ref), channel_id=1, source_target_pairs={{0,1},{1,2},{2,3},{3,0},{4,5},{5,6},{6,7},{7,4},{8,9},{9,10},{10,1... | collective-permute-start | bytes 626696 | tf_op jit(solution)/shard_map/ppermute | solution.py:78
  3.8 11.7 %collective-permute-start.3 = (bf16[272,384]{1,0:T(8,128)(2,1)S(1)}, bf16[272,384]{1,0:T(8,128)(2,1)S(1)}, u32[]{:S(2)}, u32[]{:S(2)}) collective-permute-start(bf16[272,384]{1,0:T(8,128)(2,1)S(1)} %shard_map.114.down0_ref.along0_ref.kv0_ref), channel_id=1, source_target_pairs={{0,2},{1,3},{2,0},{3,1},{4,6},{5,7},{6,4},{7,5},{8,10},{9,11},{10,... | collective-permute-start | bytes 626696 | tf_op jit(solution)/shard_map/ppermute | solution.py:78
  15.5 18.7 %collective-permute-start.4 = (bf16[256,768]{1,0:T(8,128)(2,1)S(1)}, bf16[256,768]{1,0:T(8,128)(2,1)S(1)}, u32[]{:S(2)}, u32[]{:S(2)}) collective-permute-start(bf16[256,768]{1,0:T(8,128)(2,1)S(1)} %shard_map.117.kv0_ref), channel_id=1, source_target_pairs={{0,1},{1,2},{2,3},{3,0},{4,5},{5,6},{6,7},{7,4},{8,9},{9,10},{10,1... | collective-permute-start | bytes 1179656 | tf_op jit(solution)/shard_map/ppermute | solution.py:78
  15.5 18.7 %collective-permute-start.5 = (bf16[256,768]{1,0:T(8,128)(2,1)S(1)}, bf16[256,768]{1,0:T(8,128)(2,1)S(1)}, u32[]{:S(2)}, u32[]{:S(2)}) collective-permute-start(bf16[256,768]{1,0:T(8,128)(2,1)S(1)} %shard_map.117.kv0_ref), channel_id=1, source_target_pairs={{0,2},{1,3},{2,0},{3,1},{4,6},{5,7},{6,4},{7,5},{8,10},{9,11},{10,... | collective-permute-start | bytes 1179656 | tf_op jit(solution)/shard_map/ppermute | solution.py:78
  20.6 30.9 %all-to-all-start = ((bf16[64,16,256]{2,1,0:T(8,128)(2,1)}), bf16[64,16,256]{2,1,0:T(8,128)(2,1)S(1)}, u32[]{:S(2)}, u32[]{:S(2)}) async-start(bf16[64,16,256]{2,1,0:T(8,128)(2,1)} %bitcast.15), calls=%async_computation | async-start | bytes 1048576 | tf_op jit(solution)/shard_map/all_to_all | solution.py:281
  43.9 53.9 %copy-start = (s32[64]{0:T(128)S(1)}, s32[64]{0:T(128)}, u32[]{:S(2)}) copy-start(s32[64]{0:T(128)} %plan_ref.1) | copy-start | bytes 772
  99.9 57.4 %all-to-all-start.2 = ((bf16[64,16,1024]{2,1,0:T(8,128)(2,1)}), bf16[64,16,1024]{2,1,0:T(8,128)(2,1)S(1)}, u32[]{:S(2)}, u32[]{:S(2)}) async-start(bf16[64,16,1024]{2,1,0:T(8,128)(2,1)} %shard_map.119), calls=%async_computation.2 | async-start | bytes 4194304 | tf_op jit(solution)/shard_map/all_to_all | solution.py:281
  107.2 14.5 %collective-permute-start = (bf16[256,1024]{1,0:T(8,128)(2,1)S(1)}, bf16[256,1024]{1,0:T(8,128)(2,1)S(1)}, u32[]{:S(2)}, u32[]{:S(2)}) collective-permute-start(bf16[256,1024]{1,0:T(8,128)(2,1)S(1)} %shard_map.113.kv0_ref), channel_id=1, source_target_pairs={{0,1},{1,2},{2,3},{3,0},{4,5},{5,6},{6,7},{7,4},{8,9},{9,10},{10,1... | collective-permute-start | bytes 1572872 | tf_op jit(solution)/shard_map/ppermute | solution.py:78
  110.2 23.3 %collective-permute-start.1 = (bf16[256,1024]{1,0:T(8,128)(2,1)S(1)}, bf16[256,1024]{1,0:T(8,128)(2,1)S(1)}, u32[]{:S(2)}, u32[]{:S(2)}) collective-permute-start(bf16[256,1024]{1,0:T(8,128)(2,1)S(1)} %shard_map.113.kv0_ref), channel_id=1, source_target_pairs={{0,2},{1,3},{2,0},{3,1},{4,6},{5,7},{6,4},{7,5},{8,10},{9,11},{10,... | collective-permute-start | bytes 1572872 | tf_op jit(solution)/shard_map/ppermute | solution.py:78

commit v3 on v2

--- a/solution.py
+++ b/solution.py
@@ -293,10 +293,10 @@
     lead = swap(lead.reshape(OWNERS, 16, LEAD * 256))
 
     rest = pack(ak, av, LEAD)
-    rest, _, _ = lax.optimization_barrier((rest, head1, head2))
+    rest, _ = lax.optimization_barrier((rest, head))
     rest1, rest2 = (from_previous(rest, size, s) for s in (1, 2))
     others = KEY_VALUE_HEADS - LEAD
-    other = attend(True, aq, LEAD, others, (rest, rest1, rest2), lab, tables, 30)
+    other = attend(True, aq, LEAD, others, (rest, rest1, rest2), lab, tables, 4)
     other = swap(other.reshape(OWNERS, 16, others * 256))
 
     base = pack(bk, bv, 0)

time: 160 us -> 160 us (level)
  transfers between devices with their start and end apart: 8 -> 8, of which waited for: 7 -> 4; matrix products, arithmetic and copies ran while one was open for 0% -> 0% of each run, Pallas kernels for 18% -> 18%
where the time goes in v3:
time: 160 us; the launch traced here: 159 us
  waiting for transfers between devices  50.4 us (32%)
  blocking collectives  46.1 us (29%)
  Pallas kernels  33.5 us (21%)
  starting transfers between devices  28.2 us (18%)
    all_to_all x1, blocking collectives, swap(): return lax.all_to_all(x, 'dp', split_axis=0, concat_axis=0, tiled=True)  46.1 us
    ppermute x6, waiting for transfers between devices, from_previous(): return lax.ppermute(x, 'sp', [(i, (i + step) % size) for i in range(size)])  30.6 us
    pallas_call x3, Pallas kernels, attend(): pl.pallas_call(functools.partial(attend_kernel, pieces), grid=(count,), i...  26.7 us
    all_to_all x2, starting transfers between devices, swap(): return lax.all_to_all(x, 'dp', split_axis=0, concat_axis=0, tiled=True)  20.3 us
    all_to_all x2, waiting for transfers between devices, swap(): return lax.all_to_all(x, 'dp', split_axis=0, concat_axis=0, tiled=True)  19.7 us
    ppermute x6, starting transfers between devices, from_previous(): return lax.ppermute(x, 'sp', [(i, (i + step) % size) for i in range(size)])  7.92 us
  transfers between devices with their start and end apart: 8, of which 4 were waited for; matrix products, arithmetic and copies ran while one was open for 0% of the time, Pallas kernels for 18%

profile of v3, /device:TPU:1, one launch (start us, length us, event | category | flops | bytes accessed | tf_op | source)
XLA Modules:
  0.0 159.0 jit_solution(8427657317800665147)
XLA Ops:
  0.6 1.0 shard_map.114.down0_ref.along0_ref.kv0_ref
  1.6 2.2 %collective-permute-start.2 = (bf16[272,384]{1,0:T(8,128)(2,1)S(1)}, bf16[272,384]{1,0:T(8,128)(2,1)S(1)}, u32[]{:S(2)}, u32[]{:S(2)}) collective-permute-start(bf16[272,384]{1,0:T(8,128)(2,1)S(1)} %shard_map.114.down0_ref.along0_ref.kv0_ref), channel_id=1, source_target_pairs={{0,1},{1,2},{2,3},{3,0},{4,5},{5,6},{6,7},{7,4},{8,9},{9,10},{10,1... | collective-permute-start | bytes 626696 | tf_op jit(solution)/shard_map/ppermute | solution.py:78
  3.8 2.6 %collective-permute-start.3 = (bf16[272,384]{1,0:T(8,128)(2,1)S(1)}, bf16[272,384]{1,0:T(8,128)(2,1)S(1)}, u32[]{:S(2)}, u32[]{:S(2)}) collective-permute-start(bf16[272,384]{1,0:T(8,128)(2,1)S(1)} %shard_map.114.down0_ref.along0_ref.kv0_ref), channel_id=1, source_target_pairs={{0,2},{1,3},{2,0},{3,1},{4,6},{5,7},{6,4},{7,5},{8,10},{9,11},{10,... | collective-permute-start | bytes 626696 | tf_op jit(solution)/shard_map/ppermute | solution.py:78
  6.5 1.1 shard_map.117.kv0_ref
  7.6 0.1 collective-permute-start.4
  7.7 2.2 %collective-permute-start.5 = (bf16[256,768]{1,0:T(8,128)(2,1)S(1)}, bf16[256,768]{1,0:T(8,128)(2,1)S(1)}, u32[]{:S(2)}, u32[]{:S(2)}) collective-permute-start(bf16[256,768]{1,0:T(8,128)(2,1)S(1)} %shard_map.117.kv0_ref), channel_id=1, source_target_pairs={{0,2},{1,3},{2,0},{3,1},{4,6},{5,7},{6,4},{7,5},{8,10},{9,11},{10,... | collective-permute-start | bytes 1179656 | tf_op jit(solution)/shard_map/ppermute | solution.py:78
  9.9 0.0 collective-permute-done.2.down1_ref.along1_ref.kv1_ref
  9.9 5.7 %collective-permute-done.3.down2_ref.along2_ref.kv2_ref = bf16[272,384]{1,0:T(8,128)(2,1)S(1)} collective-permute-done((bf16[272,384]{1,0:T(8,128)(2,1)S(1)}, bf16[272,384]{1,0:T(8,128)(2,1)S(1)}, u32[]{:S(2)}, u32[]{:S(2)}) %collective-permute-start.3) | collective-permute-done | bytes 208928 | tf_op jit(solution)/shard_map/ppermute | solution.py:78
  15.5 4.9 %shard_map.116 = bf16[16,4,16,256]{3,2,1,0:T(8,128)(2,1)} custom-call(s32[1]{0:T(128)} %bitcast.place_ref, bf16[256,4096]{1,0:T(8,128)(2,1)} %bitcast.13, bf16[272,384]{1,0:T(8,128)(2,1)S(1)} %shard_map.114.down0_ref.along0_ref.kv0_ref, bf16[272,384]{1,0:T(8,128)(2,1)S(1)} %collective-permute-done.2.down1_ref.along1_ref.kv1_ref, ...), custom_call_target="tpu_custom_call" | custom-call | flops 805306368 | bytes 1441792 | tf_op jit(solution)/shard_map/pallas_call | solution.py:188
  20.4 14.2 %all-to-all-start = ((bf16[64,16,256]{2,1,0:T(8,128)(2,1)}), bf16[64,16,256]{2,1,0:T(8,128)(2,1)S(1)}, u32[]{:S(2)}, u32[]{:S(2)}) async-start(bf16[64,16,256]{2,1,0:T(8,128)(2,1)} %bitcast.15), calls=%async_computation | async-start | bytes 1048576 | tf_op jit(solution)/shard_map/all_to_all | solution.py:281
  34.6 0.0 collective-permute-done.4.kv1_ref
  34.6 0.0 collective-permute-done.5.kv2_ref
  34.6 9.7 %shard_map.118 = bf16[16,4,16,768]{3,2,1,0:T(8,128)(2,1)} custom-call(s32[1]{0:T(128)} %bitcast.place_ref, bf16[256,4096]{1,0:T(8,128)(2,1)} %bitcast.14, bf16[256,768]{1,0:T(8,128)(2,1)S(1)} %shard_map.117.kv0_ref, bf16[256,768]{1,0:T(8,128)(2,1)S(1)} %collective-permute-done.4.kv1_ref, bf16[256,768]{1,0:T(8,128)(2,1)S(1)} %collective-permute-done.5.kv2_ref, ...), custom_call_target="tpu_custom_call" | custom-call | flops 9663676416 | bytes 4325376 | tf_op jit(solution)/shard_map/pallas_call | solution.py:188
  44.4 0.0 copy-start
  44.4 7.6 %all-to-all-done.lead_ref = bf16[64,16,256]{2,1,0:T(8,128)(2,1)S(1)} async-done(((bf16[64,16,256]{2,1,0:T(8,128)(2,1)}), bf16[64,16,256]{2,1,0:T(8,128)(2,1)S(1)}, u32[]{:S(2)}, u32[]{:S(2)}) %all-to-all-start) | async-done | bytes 524320 | tf_op jit(solution)/shard_map/all_to_all | solution.py:281
  51.9 46.1 %all_to_all.15.rest_ref = bf16[64,16,768]{2,1,0:T(8,128)(2,1)S(1)} all-to-all(bf16[64,16,768]{2,1,0:T(8,128)(2,1)} %bitcast.17), channel_id=1, replica_groups=mesh['dp'=64,'sp'=4] {'dp'}, dimensions={0} | all-to-all | bytes 3145728 | tf_op jit(solution)/shard_map/all_to_all | solution.py:281
  98.0 0.0 copy-done
  98.0 2.0 %shard_map.119 = bf16[64,16,1024]{2,1,0:T(8,128)(2,1)} custom-call(s32[64]{0:T(128)S(1)} %copy-done, bf16[64,16,256]{2,1,0:T(8,128)(2,1)S(1)} %all-to-all-done.lead_ref, bf16[64,16,768]{2,1,0:T(8,128)(2,1)S(1)} %all_to_all.15.rest_ref), custom_call_target="tpu_custom_call" | custom-call | tf_op jit(solution)/shard_map/pallas_call | solution.py:237
  100.0 6.1 %all-to-all-start.2 = ((bf16[64,16,1024]{2,1,0:T(8,128)(2,1)}), bf16[64,16,1024]{2,1,0:T(8,128)(2,1)S(1)}, u32[]{:S(2)}, u32[]{:S(2)}) async-start(bf16[64,16,1024]{2,1,0:T(8,128)(2,1)} %shard_map.119), calls=%async_computation.2 | async-start | bytes 4194304 | tf_op jit(solution)/shard_map/all_to_all | solution.py:281
  106.2 1.2 shard_map.113.kv0_ref
  107.3 0.3 collective-permute-start
  107.6 0.5 collective-permute-start.1
  108.1 25.0 %collective-permute-done.kv1_ref = bf16[256,1024]{1,0:T(8,128)(2,1)S(1)} collective-permute-done((bf16[256,1024]{1,0:T(8,128)(2,1)S(1)}, bf16[256,1024]{1,0:T(8,128)(2,1)S(1)}, u32[]{:S(2)}, u32[]{:S(2)}) %collective-permute-start) | collective-permute-done | bytes 524320 | tf_op jit(solution)/shard_map/ppermute | solution.py:78
  133.1 0.0 collective-permute-done.1.kv2_ref
  133.1 12.1 %shard_map.115 = bf16[256,4096]{1,0:T(8,128)(2,1)} custom-call(s32[1]{0:T(128)} %bitcast.place_ref, bf16[256,4096]{1,0:T(8,128)(2,1)} %bitcast.24, bf16[256,1024]{1,0:T(8,128)(2,1)S(1)} %shard_map.113.kv0_ref, bf16[256,1024]{1,0:T(8,128)(2,1)S(1)} %collective-permute-done.kv1_ref, bf16[256,1024]{1,0:T(8,128)(2,1)S(1)} %collective-permute-done.1.kv2_ref, ...), custom_call_target="tpu_custom_call" | custom-call | flops 3221225472 | bytes 5767168 | tf_op jit(solution)/shard_map/pallas_call | solution.py:188
  145.2 12.2 %all-to-all-done.2 = bf16[64,16,1024]{2,1,0:T(8,128)(2,1)S(1)} async-done(((bf16[64,16,1024]{2,1,0:T(8,128)(2,1)}), bf16[64,16,1024]{2,1,0:T(8,128)(2,1)S(1)}, u32[]{:S(2)}, u32[]{:S(2)}) %all-to-all-start.2) | async-done | bytes 2097184 | tf_op jit(solution)/shard_map/all_to_all | solution.py:281
  157.4 1.4 shard_map.120
Async XLA Ops:
  1.6 8.3 %collective-permute-start.2 = (bf16[272,384]{1,0:T(8,128)(2,1)S(1)}, bf16[272,384]{1,0:T(8,128)(2,1)S(1)}, u32[]{:S(2)}, u32[]{:S(2)}) collective-permute-start(bf16[272,384]{1,0:T(8,128)(2,1)S(1)} %shard_map.114.down0_ref.along0_ref.kv0_ref), channel_id=1, source_target_pairs={{0,1},{1,2},{2,3},{3,0},{4,5},{5,6},{6,7},{7,4},{8,9},{9,10},{10,1... | collective-permute-start | bytes 626696 | tf_op jit(solution)/shard_map/ppermute | solution.py:78
  3.8 11.7 %collective-permute-start.3 = (bf16[272,384]{1,0:T(8,128)(2,1)S(1)}, bf16[272,384]{1,0:T(8,128)(2,1)S(1)}, u32[]{:S(2)}, u32[]{:S(2)}) collective-permute-start(bf16[272,384]{1,0:T(8,128)(2,1)S(1)} %shard_map.114.down0_ref.along0_ref.kv0_ref), channel_id=1, source_target_pairs={{0,2},{1,3},{2,0},{3,1},{4,6},{5,7},{6,4},{7,5},{8,10},{9,11},{10,... | collective-permute-start | bytes 626696 | tf_op jit(solution)/shard_map/ppermute | solution.py:78
  7.6 27.0 %collective-permute-start.4 = (bf16[256,768]{1,0:T(8,128)(2,1)S(1)}, bf16[256,768]{1,0:T(8,128)(2,1)S(1)}, u32[]{:S(2)}, u32[]{:S(2)}) collective-permute-start(bf16[256,768]{1,0:T(8,128)(2,1)S(1)} %shard_map.117.kv0_ref), channel_id=1, source_target_pairs={{0,1},{1,2},{2,3},{3,0},{4,5},{5,6},{6,7},{7,4},{8,9},{9,10},{10,1... | collective-permute-start | bytes 1179656 | tf_op jit(solution)/shard_map/ppermute | solution.py:78
  7.7 26.9 %collective-permute-start.5 = (bf16[256,768]{1,0:T(8,128)(2,1)S(1)}, bf16[256,768]{1,0:T(8,128)(2,1)S(1)}, u32[]{:S(2)}, u32[]{:S(2)}) collective-permute-start(bf16[256,768]{1,0:T(8,128)(2,1)S(1)} %shard_map.117.kv0_ref), channel_id=1, source_target_pairs={{0,2},{1,3},{2,0},{3,1},{4,6},{5,7},{6,4},{7,5},{8,10},{9,11},{10,... | collective-permute-start | bytes 1179656 | tf_op jit(solution)/shard_map/ppermute | solution.py:78
  20.4 31.5 %all-to-all-start = ((bf16[64,16,256]{2,1,0:T(8,128)(2,1)}), bf16[64,16,256]{2,1,0:T(8,128)(2,1)S(1)}, u32[]{:S(2)}, u32[]{:S(2)}) async-start(bf16[64,16,256]{2,1,0:T(8,128)(2,1)} %bitcast.15), calls=%async_computation | async-start | bytes 1048576 | tf_op jit(solution)/shard_map/all_to_all | solution.py:281
  44.4 53.6 %copy-start = (s32[64]{0:T(128)S(1)}, s32[64]{0:T(128)}, u32[]{:S(2)}) copy-start(s32[64]{0:T(128)} %plan_ref.1) | copy-start | bytes 772
  100.0 57.4 %all-to-all-start.2 = ((bf16[64,16,1024]{2,1,0:T(8,128)(2,1)}), bf16[64,16,1024]{2,1,0:T(8,128)(2,1)S(1)}, u32[]{:S(2)}, u32[]{:S(2)}) async-start(bf16[64,16,1024]{2,1,0:T(8,128)(2,1)} %shard_map.119), calls=%async_computation.2 | async-start | bytes 4194304 | tf_op jit(solution)/shard_map/all_to_all | solution.py:281
  107.3 25.7 %collective-permute-start = (bf16[256,1024]{1,0:T(8,128)(2,1)S(1)}, bf16[256,1024]{1,0:T(8,128)(2,1)S(1)}, u32[]{:S(2)}, u32[]{:S(2)}) collective-permute-start(bf16[256,1024]{1,0:T(8,128)(2,1)S(1)} %shard_map.113.kv0_ref), channel_id=1, source_target_pairs={{0,1},{1,2},{2,3},{3,0},{4,5},{5,6},{6,7},{7,4},{8,9},{9,10},{10,1... | collective-permute-start | bytes 1572872 | tf_op jit(solution)/shard_map/ppermute | solution.py:78
  107.6 25.5 %collective-permute-start.1 = (bf16[256,1024]{1,0:T(8,128)(2,1)S(1)}, bf16[256,1024]{1,0:T(8,128)(2,1)S(1)}, u32[]{:S(2)}, u32[]{:S(2)}) collective-permute-start(bf16[256,1024]{1,0:T(8,128)(2,1)S(1)} %shard_map.113.kv0_ref), channel_id=1, source_target_pairs={{0,2},{1,3},{2,0},{3,1},{4,6},{5,7},{6,4},{7,5},{8,10},{9,11},{10,... | collective-permute-start | bytes 1572872 | tf_op jit(solution)/shard_map/ppermute | solution.py:78
